TPU v7x, 32 devices: a whole 2x2x4 slice. The times are simulated.
32 devices in a mesh: grp: 4 (over y, x), blk: 8 (over z, core).
Axes of the slice: x: 2, y: 2, z: 4, core: 2. Of those that a mesh axis runs over, the one named last changes fastest.
Arguments:
- inv_factor: bfloat16 [192, 384, 384], P(('grp', 'blk')), may hold values from -0.3125 to 0.3125
- coupling: bfloat16 [192, 384, 768], P(('grp', 'blk')), may hold values from -0.75 to 0.75
- boundary: bfloat16 [192, 768, 768], P(('grp', 'blk')), may hold values from -6 to 6
- load_int: bfloat16 [192, 384], P(('grp', 'blk')), may hold values from -6 to 6
- load_bnd: bfloat16 [192, 768], P(('grp', 'blk')), may hold values from -6 to 6
- counts: int32 [32], P(('grp', 'blk')), may hold values from 1 to 6, 128 in all
- tile_owner: int32 [192, 36, 1], P(('grp', 'blk')), may hold values from 0 to 31; in each aligned block of 216 rows (0 to 215, 216 to 431, ..., all dimensions but the last counted through in order) at most 10 rows name the same one
- tile_slot: int32 [192, 36], P(('grp', 'blk')), may hold values from 0 to 63
- vec_owner: int32 [192, 6, 1], P(('grp', 'blk')), may hold values from 0 to 31; in each aligned block of 36 rows (0 to 35, 36 to 71, ..., all dimensions but the last counted through in order) at most 2 rows name the same one
- vec_slot: int32 [192, 6], P(('grp', 'blk')), may hold values from 0 to 15
Outputs:
- assembled: float32 [2048, 128, 128], P(('grp', 'blk'))
- loads: float32 [512, 128], P(('grp', 'blk'))
Inputs may be any that keep to these rules, and one draw needn't show every extreme that they name: `tile_owner`: among the 216 rows of one device, no owner is named by more than 10 tiles. `vec_owner`: among the 36 rows of one device, no owner is named by more than 2 load blocks.
All inputs are finite; a program needn't handle non-finite values. No bound on the sum of `counts` on one device may be relied on, other than what follows from the above.
Results may differ from a plain program's by a relative error of at most 0.004.
Values may be sent and summed in bfloat16 or wider, within the bound.
A program may use at most 128 MiB of HBM per device.

v0:
```python
import jax
import jax.numpy as jnp
from jax import lax
from jax.sharding import PartitionSpec as P

BLOCK_UNKNOWNS = 128
SLOT_DEV = 64
VSLOT_DEV = 16


def placement(owner, peers, room):
    count = owner.shape[0]
    hits = (owner[:, None] == jnp.arange(peers, dtype=jnp.int32)[None, :]).astype(jnp.int32)
    rank = jnp.sum(jnp.cumsum(hits, axis=0) * hits, axis=1) - 1
    target = owner * room + rank
    return (
        jnp.full((peers * room,), count, jnp.int32)
        .at[target]
        .set(jnp.arange(count, dtype=jnp.int32))
    )


def packed(rows, slots, source):
    padded_rows = jnp.concatenate([rows, jnp.zeros((1, rows.shape[1]), rows.dtype)], axis=0)
    padded_ids = jnp.concatenate([slots, jnp.full((1,), -1, jnp.int32)])
    return (padded_rows[source], padded_ids[source])


def summed(rows, ids, count):
    select = (ids[None, :] == jnp.arange(count, dtype=jnp.int32)[:, None]).astype(rows.dtype)
    return jnp.dot(select, rows, preferred_element_type=jnp.float32)


def shards(
    inv_factor,
    coupling,
    boundary,
    load_int,
    load_bnd,
    counts,
    tile_owner,
    tile_slot,
    vec_owner,
    vec_slot,
):
    emax = inv_factor.shape[0]
    nb = boundary.shape[1]
    tile = BLOCK_UNKNOWNS
    tiles = nb // tile
    element_groups = lax.axis_size("grp")
    columns = lax.axis_size("blk")
    peers = element_groups * columns
    ntiles = emax * tiles * tiles
    room = max(2, 3 * ntiles // (2 * peers))
    vroom = max(2, 3 * emax * tiles // (2 * peers))

    def condense(slot_index, carry):
        stiffness_matrices, load_vectors = carry
        factor = lax.dynamic_index_in_dim(inv_factor, slot_index, 0, keepdims=False)
        couple = lax.dynamic_index_in_dim(coupling, slot_index, 0, keepdims=False)
        bound = lax.dynamic_index_in_dim(boundary, slot_index, 0, keepdims=False)
        inner = lax.dynamic_index_in_dim(load_int, slot_index, 0, keepdims=False)
        outer = lax.dynamic_index_in_dim(load_bnd, slot_index, 0, keepdims=False)
        coupled = jnp.dot(factor, couple, preferred_element_type=jnp.float32).astype(jnp.bfloat16)
        product = lax.dot_general(
            coupled, coupled, (((0,), (0,)), ((), ())), preferred_element_type=jnp.float32
        )
        schur = (bound.astype(jnp.float32) - product).astype(jnp.bfloat16)
        pulled = jnp.dot(factor, inner, preferred_element_type=jnp.float32).astype(jnp.bfloat16)
        condensed = (
            outer.astype(jnp.float32) - jnp.dot(pulled, coupled, preferred_element_type=jnp.float32)
        ).astype(jnp.bfloat16)
        stiffness_matrices = lax.dynamic_update_index_in_dim(
            stiffness_matrices, schur, slot_index, 0
        )
        load_vectors = lax.dynamic_update_index_in_dim(load_vectors, condensed, slot_index, 0)
        return (stiffness_matrices, load_vectors)

    start_offset = (jnp.zeros((emax, nb, nb), jnp.bfloat16), jnp.zeros((emax, nb), jnp.bfloat16))
    stiffness_matrices, load_vectors = lax.fori_loop(0, counts[0], condense, start_offset)
    pieces = (
        stiffness_matrices.reshape(emax, tiles, tile, tiles, tile)
        .transpose(0, 1, 3, 2, 4)
        .reshape(ntiles, tile * tile)
    )
    blocks = load_vectors.reshape(emax * tiles, tile)
    source = placement(tile_owner.reshape(-1), peers, room)
    vsource = placement(vec_owner.reshape(-1), peers, vroom)
    send_tiles, send_ids = packed(pieces, tile_slot.reshape(-1), source)
    send_blocks, send_vids = packed(blocks, vec_slot.reshape(-1), vsource)
    received_tiles, got_ids, got_blocks, got_vids = (
        lax.all_to_all(send_tiles, ("grp", "blk"), split_axis=0, concat_axis=0, tiled=True),
        lax.all_to_all(send_ids, ("grp", "blk"), split_axis=0, concat_axis=0, tiled=True),
        lax.all_to_all(send_blocks, ("grp", "blk"), split_axis=0, concat_axis=0, tiled=True),
        lax.all_to_all(send_vids, ("grp", "blk"), split_axis=0, concat_axis=0, tiled=True),
    )
    assembled = summed(received_tiles, got_ids, SLOT_DEV).reshape(SLOT_DEV, tile, tile)
    loads = summed(got_blocks, got_vids, VSLOT_DEV)
    return (assembled, loads)


def solution(mesh):
    in_specs = (
        P(("grp", "blk"), None, None),
        P(("grp", "blk"), None, None),
        P(("grp", "blk"), None, None),
        P(("grp", "blk"), None),
        P(("grp", "blk"), None),
        P(("grp", "blk")),
        P(("grp", "blk"), None, None),
        P(("grp", "blk"), None),
        P(("grp", "blk"), None, None),
        P(("grp", "blk"), None),
    )
    out_specs = (P(("grp", "blk"), None, None), P(("grp", "blk"), None))
    return jax.shard_map(shards, mesh=mesh, in_specs=in_specs, out_specs=out_specs, check_vma=False)
```

profile of v0, /device:TPU:11, one launch (start us, length us, event | category | flops | bytes accessed | tf_op | source)
XLA Modules:
  0.0 552.4 jit_solution(4628527389057809539)
XLA Ops:
  4.9 6.3 %all-to-all-start.2 = ((s32[32,2,1]{1,2,0:T(1,128)}), s32[32,2,1]{1,2,0:T(1,128)S(1)}, u32[]{:S(2)}, u32[]{:S(2)}) async-start(s32[32,2,1]{1,2,0:T(1,128)} %bitcast.14), calls=%async_computation.2 | async-start | bytes 32768 | tf_op jit(solution)/shard_map/all_to_all | solution.py:95
  13.9 1.3 scatter_custom_fusion
  15.2 2.4 gather_fusion
  18.4 5.8 %all-to-all-start = ((s32[32,10,1]{1,2,0:T(1,128)}), s32[32,10,1]{1,2,0:T(1,128)S(1)}, u32[]{:S(2)}, u32[]{:S(2)}) async-start(s32[32,10,1]{1,2,0:T(1,128)} %bitcast.7), calls=%async_computation | async-start | bytes 32768 | tf_op jit(solution)/shard_map/all_to_all | solution.py:93
  24.3 3.3 broadcast_in_dim.40
  27.6 38.9 %while.12 = (s32[]{:T(128)}, bf16[6,768,768]{2,1,0:T(8,128)(2,1)}, bf16[6,768]{1,0:T(8,128)(2,1)S(1)}, s32[]{:T(128)}, bf16[6,768,768]{2,1,0:T(8,128)(2,1)}, /*i...) while((s32[]{:T(128)}, bf16[6,768,768]{2,1,0:T(8,128)(2,1)}, ...), condition=%wide.region_5.6_spmd, body=%wide.region_4.5_spmd.sunk | while | flops 682428672 | bytes 5926571 | solution.py:80
  30.2 1.6 convolution_convert_fusion.2
  32.1 3.1 fusion.53
  37.8 1.6 convolution_convert_fusion.2
  39.7 3.1 fusion.53
  43.5 1.2 convolution_reduce_fusion.4
  45.4 1.6 convolution_convert_fusion.2
  47.4 3.1 fusion.53
  51.2 1.2 convolution_reduce_fusion.4
  53.1 1.6 convolution_convert_fusion.2
  55.1 3.1 fusion.53
  58.9 1.2 convolution_reduce_fusion.4
  60.8 1.6 convolution_convert_fusion.2
  62.7 3.1 fusion.53
  66.5 1.2 gather_fusion.3
  67.8 13.5 %all-to-all-start.3 = ((bf16[32,2,128]{2,1,0:T(2,128)(2,1)}), bf16[32,2,128]{2,1,0:T(2,128)(2,1)S(1)}, u32[]{:S(2)}, u32[]{:S(2)}) async-start(bf16[32,2,128]{2,1,0:T(2,128)(2,1)} %bitcast.15), calls=%async_computation.3 | async-start | bytes 32768 | tf_op jit(solution)/shard_map/all_to_all | solution.py:94
  81.3 15.3 %reshape.121 = bf16[6,6,128,6,128]{4,3,2,1,0:T(8,128)(2,1)} reshape(bf16[6,768,768]{2,1,0:T(8,128)(2,1)} %get-tuple-element.51) | data formatting | bytes 14155776 | tf_op jit(solution)/shard_map/reshape | solution.py:82
  96.6 8.7 %copy.22 = bf16[6,6,6,128,128]{4,3,2,1,0:T(8,128)(2,1)} copy(bf16[6,6,6,128,128]{4,2,3,1,0:T(8,128)(2,1)} %bitcast.89) | data formatting | bytes 14155776 | tf_op jit(solution)/shard_map/transpose | solution.py:83
  105.2 9.6 %copy.37 = bf16[27,8,128,128]{3,1,2,0:T(8,128)(2,1)S(1)} copy(bf16[27,8,128,128]{3,2,1,0:T(8,128)(2,1)} %bitcast.91) | data formatting | bytes 14155776
  114.8 3.8 concatenate.13
  118.6 31.4 %gather_fusion.1 = bf16[320,16384]{1,0:T(8,128)(2,1)} fusion(bf16[217,16384]{1,0:T(8,128)(2,1)} %concatenate.13, s32[1024]{0:T(1024)S(1)} %pad_clamp_fusion.1), kind=kCustom, calls=%fused_computation.1 | custom fusion | bytes 20972800 | tf_op jit(solution)/shard_map/gather | solution.py:26
  150.0 12.7 %all_to_all.30 = bf16[32,10,16384]{2,1,0:T(8,128)(2,1)} reshape(bf16[320,16384]{1,0:T(8,128)(2,1)} %gather_fusion.1) | data formatting | bytes 20971520 | tf_op jit(solution)/shard_map/all_to_all | solution.py:92
  162.6 5.9 %all-to-all-start.1 = ((bf16[32,10,16384]{2,1,0:T(8,128)(2,1)}), bf16[32,10,16384]{2,1,0:T(8,128)(2,1)}, u32[]{:S(2)}, u32[]{:S(2)}) async-start(bf16[32,10,16384]{2,1,0:T(8,128)(2,1)} %all_to_all.30), calls=%async_computation.1 | async-start | bytes 33554432 | tf_op jit(solution)/shard_map/all_to_all | solution.py:92
  171.4 357.3 %all-to-all-done.1 = bf16[32,10,16384]{2,1,0:T(8,128)(2,1)} async-done(((bf16[32,10,16384]{2,1,0:T(8,128)(2,1)}), bf16[32,10,16384]{2,1,0:T(8,128)(2,1)}, u32[]{:S(2)}, u32[]{:S(2)}) %all-to-all-start.1) | async-done | bytes 10485792 | tf_op jit(solution)/shard_map/all_to_all | solution.py:92
  528.7 13.0 %all_to_all.32 = bf16[320,16384]{1,0:T(8,128)(2,1)} reshape(bf16[32,10,16384]{2,1,0:T(8,128)(2,1)} %all-to-all-done.1) | data formatting | bytes 20971520 | tf_op jit(solution)/shard_map/all_to_all | solution.py:92
  541.8 6.2 %fusion.13 = f32[64,128,128]{2,0,1:T(8,128)S(1)} fusion(s32[320]{0:T(512)S(1)} %eq.74, bf16[320,16384]{1,0:T(8,128)(2,1)} %all_to_all.32), kind=kOutput, calls=%fused_computation.25 | convolution fusion | flops 671109120 | bytes 14681344 | tf_op jit(solution)/shard_map/dot_general | solution.py:31
  547.9 4.4 copy.25
  (78 shorter events, 17.9 us)
Async XLA Ops:
  4.9 13.5 %all-to-all-start.2 = ((s32[32,2,1]{1,2,0:T(1,128)}), s32[32,2,1]{1,2,0:T(1,128)S(1)}, u32[]{:S(2)}, u32[]{:S(2)}) async-start(s32[32,2,1]{1,2,0:T(1,128)} %bitcast.14), calls=%async_computation.2 | async-start | bytes 32768 | tf_op jit(solution)/shard_map/all_to_all | solution.py:95
  18.4 49.4 %all-to-all-start = ((s32[32,10,1]{1,2,0:T(1,128)}), s32[32,10,1]{1,2,0:T(1,128)S(1)}, u32[]{:S(2)}, u32[]{:S(2)}) async-start(s32[32,10,1]{1,2,0:T(1,128)} %bitcast.7), calls=%async_computation | async-start | bytes 32768 | tf_op jit(solution)/shard_map/all_to_all | solution.py:93
  67.8 94.9 %all-to-all-start.3 = ((bf16[32,2,128]{2,1,0:T(2,128)(2,1)}), bf16[32,2,128]{2,1,0:T(2,128)(2,1)S(1)}, u32[]{:S(2)}, u32[]{:S(2)}) async-start(bf16[32,2,128]{2,1,0:T(2,128)(2,1)} %bitcast.15), calls=%async_computation.3 | async-start | bytes 32768 | tf_op jit(solution)/shard_map/all_to_all | solution.py:94
  162.6 366.1 %all-to-all-start.1 = ((bf16[32,10,16384]{2,1,0:T(8,128)(2,1)}), bf16[32,10,16384]{2,1,0:T(8,128)(2,1)}, u32[]{:S(2)}, u32[]{:S(2)}) async-start(bf16[32,10,16384]{2,1,0:T(8,128)(2,1)} %all_to_all.30), calls=%async_computation.1 | async-start | bytes 33554432 | tf_op jit(solution)/shard_map/all_to_all | solution.py:92
where the time goes:
time: 560 us; the launch traced here: 552 us
  waiting for transfers between devices  357 us (64%)
  local copies, waits for them, and re-layouts  113 us (20%)
  matrix products  37.6 us (7%)
  starting transfers between devices  31.6 us (6%)
  other arithmetic  7.73 us (1%)
    all_to_all x1, waiting for transfers between devices, shards(): lax.all_to_all(send_tiles, ('grp', 'blk'), split_axis=0, concat_axis=0, t...  357 us
    gather x4, local copies, waits for them, and re-layouts, packed(): return (padded_rows[source], padded_ids[source])  35.8 us
    all_to_all x2, local copies, waits for them, and re-layouts, shards(): lax.all_to_all(send_tiles, ('grp', 'blk'), split_axis=0, concat_axis=0, t...  25.7 us
    dot_general x5, matrix products, condense(): lax.dot_general(coupled, coupled, (((0,), (0,)), ((), ())), preferred_ele...  15.6 us
    reshape x1, local copies, waits for them, and re-layouts, shards(): stiffness_matrices.reshape(emax, tiles, tile, tiles, tile)  15.3 us
    unnamed x2, local copies, waits for them, and re-layouts  14 us
    all_to_all x1, starting transfers between devices, shards(): lax.all_to_all(send_blocks, ('grp', 'blk'), split_axis=0, concat_axis=0,...  13.5 us
  transfers between devices with their start and end apart: 4, of which 1 were waited for; matrix products, arithmetic and copies ran while one was open for 21% of the time, Pallas kernels for 0%

commit v1 on v0

v1 whole, which is shorter than its diff:
```python
import functools

import jax
import jax.numpy as jnp
from jax import lax
from jax.experimental import pallas as pl
from jax.experimental.pallas import tpu as pltpu
from jax.sharding import PartitionSpec as P

BLOCK_UNKNOWNS = 128
SLOT_DEV = 64
VSLOT_DEV = 16
LANES = 128
MESH = pl.DeviceIdType.MESH


def ranks(owner):
    count = owner.shape[0]
    same = owner[:, None] == owner[None, :]
    before = jnp.arange(count)[None, :] < jnp.arange(count)[:, None]
    return jnp.sum((same & before).astype(jnp.int32), axis=1)


def slot_table(owner, rank, slot, live, peers):
    hit = (owner[None, None, :] == jnp.arange(peers, dtype=jnp.int32)[:, None, None]) & (
        rank[None, None, :] == jnp.arange(LANES, dtype=jnp.int32)[None, :, None]
    )
    return jnp.max(jnp.where(hit & live[None, None, :], slot[None, None, :], -1), axis=2)


def condense_kernel(
    emax,
    tiles,
    counts,
    pos,
    vpos,
    factor_ref,
    couple_ref,
    bound_ref,
    inner_ref,
    outer_ref,
    ids_ref,
    send_ref,
    aux_ref,
    held,
    sems,
):
    tile = BLOCK_UNKNOWNS
    e = pl.program_id(0)
    live = counts[0]
    slot = lax.rem(e, 2)

    def drain(which):
        for t in range(tiles * tiles):
            pltpu.make_async_copy(held.at[which, t], send_ref.at[0], sems.at[which, t]).wait()

    @pl.when(e == 0)
    def _():
        aux_ref[...] = ids_ref[...]

    @pl.when(e < live)
    def _():
        factor = factor_ref[0]
        coupled = jnp.dot(factor, couple_ref[0], preferred_element_type=jnp.float32).astype(
            jnp.bfloat16
        )

        def row(ref):
            whole = ref[...].astype(jnp.float32)
            mine = lax.broadcasted_iota(jnp.int32, whole.shape, 0) == e
            return jnp.sum(jnp.where(mine, whole, 0.0), axis=0, keepdims=True)

        inner = jnp.broadcast_to(row(inner_ref), (8, inner_ref.shape[1])).astype(jnp.bfloat16)
        pulled = lax.dot_general(
            inner, factor, (((1,), (1,)), ((), ())), preferred_element_type=jnp.float32
        ).astype(jnp.bfloat16)
        drop = jnp.dot(pulled, coupled, preferred_element_type=jnp.float32)[0:1]
        condensed = (row(outer_ref) - drop).astype(jnp.bfloat16).astype(jnp.float32)
        for a in range(tiles):
            aux_ref[pl.ds(vpos[e * tiles + a], 1), :] = condensed[:, a * tile : (a + 1) * tile]

        product = lax.dot_general(
            coupled, coupled, (((0,), (0,)), ((), ())), preferred_element_type=jnp.float32
        )

        @pl.when(e >= 2)
        def _():
            drain(slot)

        for a in range(tiles):
            rows = slice(a * tile, (a + 1) * tile)
            for b in range(tiles):
                cols = slice(b * tile, (b + 1) * tile)
                t = a * tiles + b
                held[slot, t] = (
                    bound_ref[0, rows, cols].astype(jnp.float32) - product[rows, cols]
                ).astype(jnp.bfloat16)
                pltpu.make_async_copy(
                    held.at[slot, t],
                    send_ref.at[pos[e * tiles * tiles + t]],
                    sems.at[slot, t],
                ).start()

    @pl.when(e == emax - 1)
    def _():
        @pl.when(live >= 2)
        def _():
            drain(lax.rem(live, 2))

        drain(lax.rem(live + 1, 2))


def exchange_kernel(peers, columns, room, auxrows, send, aux, recv, auxrecv, sems, auxsems, own):
    me = lax.axis_index("grp") * columns + lax.axis_index("blk")

    def coords(d):
        return (d // columns, d % columns)

    barrier = pltpu.get_barrier_semaphore()

    @pl.loop(1, peers)
    def _(k):
        pl.semaphore_signal(
            barrier, inc=1, device_id=coords((me + k) % peers), device_id_type=MESH
        )

    pl.semaphore_wait(barrier, peers - 1)

    def tile_copy(k):
        d = (me + k) % peers
        return pltpu.make_async_remote_copy(
            src_ref=send.at[pl.ds(d * room, room)],
            dst_ref=recv.at[pl.ds(me * room, room)],
            send_sem=sems.at[0, k],
            recv_sem=sems.at[1, k],
            device_id=coords(d),
            device_id_type=MESH,
        )

    def aux_copy(k):
        d = (me + k) % peers
        return pltpu.make_async_remote_copy(
            src_ref=aux.at[pl.ds(d * auxrows, auxrows)],
            dst_ref=auxrecv.at[pl.ds(me * auxrows, auxrows)],
            send_sem=auxsems.at[0, k],
            recv_sem=auxsems.at[1, k],
            device_id=coords(d),
            device_id_type=MESH,
        )

    @pl.loop(1, peers)
    def _(k):
        tile_copy(k).start()
        aux_copy(k).start()

    mine = pltpu.make_async_copy(
        send.at[pl.ds(me * room, room)], recv.at[pl.ds(me * room, room)], own.at[0]
    )
    auxmine = pltpu.make_async_copy(
        aux.at[pl.ds(me * auxrows, auxrows)], auxrecv.at[pl.ds(me * auxrows, auxrows)], own.at[1]
    )
    mine.start()
    auxmine.start()
    mine.wait()
    auxmine.wait()

    @pl.loop(1, peers)
    def _(k):
        tile_copy(k).wait()
        aux_copy(k).wait()


def sum_kernel(
    peers, group, room, vroom, auxrows, ids, vids, recv_ref, aux_ref, out_ref, loads_ref
):
    step = pl.program_id(0)

    @pl.when(step == 0)
    def _():
        out_ref[...] = jnp.zeros_like(out_ref)
        loads_ref[...] = jnp.zeros_like(loads_ref)

        @pl.loop(0, peers)
        def _(p):
            for v in range(vroom):
                target = vids[p * vroom + v]

                @pl.when(target >= 0)
                def _():
                    loads_ref[pl.ds(target, 1), :] += aux_ref[pl.ds(p * auxrows + v, 1), :]

    @pl.loop(0, group * room)
    def _(t):
        target = ids[step * group * room + t]

        @pl.when(target >= 0)
        def _():
            out_ref[target] += recv_ref[t].astype(jnp.float32)


def shards(
    inv_factor,
    coupling,
    boundary,
    load_int,
    load_bnd,
    counts,
    tile_owner,
    tile_slot,
    vec_owner,
    vec_slot,
):
    emax, ni, _ = inv_factor.shape
    nb = boundary.shape[1]
    tile = BLOCK_UNKNOWNS
    tiles = nb // tile
    columns = lax.axis_size("blk")
    peers = lax.axis_size("grp") * columns
    ntiles = emax * tiles * tiles
    room = max(2, 3 * ntiles // (2 * peers))
    vroom = max(2, 3 * emax * tiles // (2 * peers))
    vrows = -(-vroom // 8) * 8
    auxrows = vrows + 8

    owner = tile_owner.reshape(-1)
    vowner = vec_owner.reshape(-1)
    rank, vrank = ranks(owner), ranks(vowner)
    pos = owner * room + rank
    vpos = vowner * auxrows + vrank
    live = jnp.arange(ntiles) < counts[0] * (tiles * tiles)
    vlive = jnp.arange(emax * tiles) < counts[0] * tiles
    ids = slot_table(owner, rank, tile_slot.reshape(-1), live, peers)
    vids = slot_table(vowner, vrank, vec_slot.reshape(-1), vlive, peers)
    at = lax.broadcasted_iota(jnp.int32, (1, auxrows, 1), 1)
    table = jnp.where(
        at == vrows, ids[:, None, :], jnp.where(at == vrows + 1, vids[:, None, :], 0)
    )
    table = table.astype(jnp.float32).reshape(peers * auxrows, LANES)

    def element(e, cnt, *_):
        return (jnp.minimum(e, cnt[0] - 1), 0, 0)

    def whole(*_):
        return (0, 0)

    send, aux = pl.pallas_call(
        functools.partial(condense_kernel, emax, tiles),
        grid_spec=pltpu.PrefetchScalarGridSpec(
            num_scalar_prefetch=3,
            grid=(emax,),
            in_specs=[
                pl.BlockSpec((1, ni, ni), element),
                pl.BlockSpec((1, ni, nb), element),
                pl.BlockSpec((1, nb, nb), element),
                pl.BlockSpec((emax, ni), whole),
                pl.BlockSpec((emax, nb), whole),
                pl.BlockSpec((peers * auxrows, LANES), whole),
            ],
            out_specs=[
                pl.BlockSpec(memory_space=pl.ANY),
                pl.BlockSpec((peers * auxrows, LANES), whole),
            ],
            scratch_shapes=[
                pltpu.VMEM((2, tiles * tiles, tile, tile), jnp.bfloat16),
                pltpu.SemaphoreType.DMA((2, tiles * tiles)),
            ],
        ),
        out_shape=[
            jax.ShapeDtypeStruct((peers * room, tile, tile), jnp.bfloat16),
            jax.ShapeDtypeStruct((peers * auxrows, LANES), jnp.float32),
        ],
        compiler_params=pltpu.CompilerParams(
            dimension_semantics=("arbitrary",), vmem_limit_bytes=40 * 1024 * 1024
        ),
        name="condense",
    )(counts, pos, vpos, inv_factor, coupling, boundary, load_int, load_bnd, table)

    recv, auxrecv = pl.pallas_call(
        functools.partial(exchange_kernel, peers, columns, room, auxrows),
        in_specs=[pl.BlockSpec(memory_space=pl.ANY)] * 2,
        out_specs=[pl.BlockSpec(memory_space=pl.ANY)] * 2,
        out_shape=[
            jax.ShapeDtypeStruct((peers * room, tile, tile), jnp.bfloat16),
            jax.ShapeDtypeStruct((peers * auxrows, LANES), jnp.float32),
        ],
        scratch_shapes=[
            pltpu.SemaphoreType.DMA((2, peers)),
            pltpu.SemaphoreType.DMA((2, peers)),
            pltpu.SemaphoreType.DMA((2,)),
        ],
        compiler_params=pltpu.CompilerParams(collective_id=0, has_side_effects=True),
        name="exchange",
    )(send, aux)

    got = auxrecv.reshape(peers, auxrows, LANES)
    got_ids = got[:, vrows, :room].astype(jnp.int32).reshape(-1)
    got_vids = got[:, vrows + 1, :vroom].astype(jnp.int32).reshape(-1)
    group = 4 if peers % 4 == 0 else 1

    assembled, loads = pl.pallas_call(
        functools.partial(sum_kernel, peers, group, room, vroom, auxrows),
        grid_spec=pltpu.PrefetchScalarGridSpec(
            num_scalar_prefetch=2,
            grid=(peers // group,),
            in_specs=[
                pl.BlockSpec((group * room, tile, tile), lambda s, *_: (s, 0, 0)),
                pl.BlockSpec((peers * auxrows, LANES), whole),
            ],
            out_specs=[
                pl.BlockSpec((SLOT_DEV, tile, tile), lambda s, *_: (0, 0, 0)),
                pl.BlockSpec((VSLOT_DEV, LANES), whole),
            ],
        ),
        out_shape=[
            jax.ShapeDtypeStruct((SLOT_DEV, tile, tile), jnp.float32),
            jax.ShapeDtypeStruct((VSLOT_DEV, LANES), jnp.float32),
        ],
        compiler_params=pltpu.CompilerParams(
            dimension_semantics=("arbitrary",), vmem_limit_bytes=40 * 1024 * 1024
        ),
        name="assemble",
    )(got_ids, got_vids, recv, auxrecv)
    return (assembled, loads)


def solution(mesh):
    in_specs = (
        P(("grp", "blk"), None, None),
        P(("grp", "blk"), None, None),
        P(("grp", "blk"), None, None),
        P(("grp", "blk"), None),
        P(("grp", "blk"), None),
        P(("grp", "blk")),
        P(("grp", "blk"), None, None),
        P(("grp", "blk"), None),
        P(("grp", "blk"), None, None),
        P(("grp", "blk"), None),
    )
    out_specs = (P(("grp", "blk"), None, None), P(("grp", "blk"), None))
    return jax.shard_map(shards, mesh=mesh, in_specs=in_specs, out_specs=out_specs, check_vma=False)
```

time: 560 us -> 292 us (0.52); the launches traced: 552 us -> 291 us
  waiting for transfers between devices: 357 us -> 0 us
  Pallas kernels: 0 us -> 268 us
  local copies, waits for them, and re-layouts: 113 us -> 17.4 us
  matrix products: 37.6 us -> 0 us
  starting transfers between devices: 31.6 us -> 0 us
    all_to_all x4 -> x0, waiting for transfers between devices: 357 us -> none  [the longest x1 357 us: shards(): lax.all_to_all(send_tiles, ('grp', 'blk'), split_axis=0, concat_axis=0, t...]
    pallas_call x0 -> x3, Pallas kernels: none -> 268 us  [the longest x1 247 us: shards(): pl.pallas_call(functools.partial(exchange_kernel, peers, columns, room, a...]
    dot_general x22 -> x0, matrix products: 37.6 us -> none  [the longest x5 15.6 us: condense(): lax.dot_general(coupled, coupled, (((0,), (0,)), ((), ())), preferred_ele...]
    gather x4 -> x0, local copies, waits for them, and re-layouts: 35.8 us -> none  [packed(): return (padded_rows[source], padded_ids[source])]
    all_to_all x4 -> x0, starting transfers between devices: 31.6 us -> none  [the longest x1 13.5 us: shards(): lax.all_to_all(send_blocks, ('grp', 'blk'), split_axis=0, concat_axis=0,...]
    all_to_all x5 -> x0, local copies, waits for them, and re-layouts: 27.6 us -> none  [the longest x2 25.7 us: shards(): lax.all_to_all(send_tiles, ('grp', 'blk'), split_axis=0, concat_axis=0, t...]
    reshape x4 -> x2, local copies, waits for them, and re-layouts: 16.8 us -> 0.16 us  [the longest x1 0.08 us: shards(): owner = tile_owner.reshape(-1)]
    transpose x1 -> x0, local copies, waits for them, and re-layouts: 8.68 us -> none  [shards(): pieces = stiffness_matrices.reshape(emax, tiles, tile, tiles, tile).trans...]
  transfers between devices with their start and end apart: 4 -> 0, of which waited for: 1 -> 0; matrix products, arithmetic and copies ran while one was open for 21% -> 0% of each run, Pallas kernels for 0% -> 0%
where the time goes in v1:
time: 292 us; the launch traced here: 291 us
  Pallas kernels  268 us (92%)
  local copies, waits for them, and re-layouts  17.4 us (6%)
  other arithmetic  4.02 us (1%)
    pallas_call x1, Pallas kernels, shards(): pl.pallas_call(functools.partial(exchange_kernel, peers, columns, room, a...  247 us
    unnamed x16, local copies, waits for them, and re-layouts  13.5 us
    pallas_call x1, Pallas kernels, shards(): pl.pallas_call(functools.partial(condense_kernel, emax, tiles), grid_spec...  12.1 us
    pallas_call x1, Pallas kernels, shards(): pl.pallas_call(functools.partial(sum_kernel, peers, group, room, vroom, a...  9.03 us

profile of v1, /device:TPU:11, one launch (start us, length us, event | category | flops | bytes accessed | tf_op | source)
XLA Modules:
  0.0 291.3 jit_solution(3140743165730868035)
XLA Ops:
  1.3 0.8 broadcast_in_dim.101
  2.1 0.8 broadcast_in_dim.93
  2.9 0.1 broadcast_in_dim.99
  3.0 0.1 broadcast_in_dim.91
  3.0 0.7 reduce
  3.8 0.1 reshape.152
  3.8 0.2 convert_reduce_fusion
  4.0 0.7 reduce.1
  4.7 0.1 reshape.153
  4.8 0.2 convert_reduce_fusion.1
  5.0 0.1 iota_compare_fusion.4
  5.1 0.1 iota_compare_fusion.3
  5.2 0.3 select_reduce_fusion.1
  5.5 0.1 iota_compare_fusion.1
  5.6 1.4 select_reduce_fusion
  7.0 0.2 fusion.1.ids_ref
  7.2 0.0 copy-start.1
  7.3 3.0 %copy-done.1 = bf16[6,768,768]{2,1,0:T(8,128)(2,1)S(1)} copy-done((bf16[6,768,768]{2,1,0:T(8,128)(2,1)S(1)}, bf16[6,768,768]{2,1,0:T(8,128)(2,1)}, u32[]{:S(2)}) %copy-start.1) | copy-done | bytes 7077912
  10.3 2.0 copy-done.2
  12.3 1.5 copy-done.3
  13.7 0.7 copy-done.6
  14.4 0.7 copy-done.7
  15.1 12.1 %condense.1 = (bf16[320,128,128]{2,1,0:T(8,128)(2,1)}, f32[512,128]{1,0:T(8,128)S(1)}) custom-call(s32[1]{0:T(128)S(6)} %copy.19.counts, s32[216]{0:T(256)S(1)} %multiply_add_fusion.pos, s32[36]{0:T(128)S(1)} %multiply_add_fusion.1.vpos, bf16[6,384,384]{2,1,0:T(8,128)(2,1)S(1)} %copy-done.3, bf16[6,384,768]{2,1,0:T(8,128)(2,1)S(1)} %copy-done.2, ...), custom_call_target="tpu_custom_call" | custom-call | tf_op jit(solution)/shard_map/condense/pallas_call | solution.py:246
  27.2 0.7 copy-done.5
  27.9 247.3 %exchange.1 = (bf16[320,128,128]{2,1,0:T(8,128)(2,1)}, f32[512,128]{1,0:T(8,128)}) custom-call(bf16[320,128,128]{2,1,0:T(8,128)(2,1)} %get-tuple-element.6.send, f32[512,128]{1,0:T(8,128)} %copy-done.5), custom_call_target="tpu_custom_call" | custom-call | tf_op jit(solution)/shard_map/exchange/pallas_call | solution.py:278
  275.2 0.9 slice.8
  276.2 0.1 convert_element_type.28.ids
  276.3 0.9 slice.9
  277.2 0.1 convert_element_type.30.vids
  277.3 4.0 %copy-done = bf16[320,128,128]{2,1,0:T(8,128)(2,1)S(1)} copy-done((bf16[320,128,128]{2,1,0:T(8,128)(2,1)S(1)}, bf16[320,128,128]{2,1,0:T(8,128)(2,1)}, u32[]{:S(2)}) %copy-start) | copy-done | bytes 10485784
  281.3 0.9 copy-done.4
  282.3 9.0 %assemble.1 = (f32[64,128,128]{2,1,0:T(8,128)}, f32[16,128]{1,0:T(8,128)}) custom-call(s32[320]{0:T(512)S(1)} %convert_element_type.28.ids, s32[64]{0:T(128)S(1)} %convert_element_type.30.vids, bf16[320,128,128]{2,1,0:T(8,128)(2,1)S(1)} %copy-done, f32[512,128]{1,0:T(8,128)S(1)} %copy-done.4), custom_call_target="tpu_custom_call" | custom-call | tf_op jit(solution)/shard_map/assemble/pallas_call | solution.py:300
  (18 shorter events, 0.1 us)
Async XLA Ops:
  7.2 3.0 %copy-start.1 = (bf16[6,768,768]{2,1,0:T(8,128)(2,1)S(1)}, bf16[6,768,768]{2,1,0:T(8,128)(2,1)}, u32[]{:S(2)}) copy-start(bf16[6,768,768]{2,1,0:T(8,128)(2,1)} %bound_ref.1) | copy-start | bytes 21233668
  10.3 2.0 copy-start.2
  12.3 1.5 copy-start.3
  13.7 0.7 copy-start.6
  14.4 0.7 copy-start.7
  27.2 0.7 copy-start.5
  277.3 4.0 %copy-start = (bf16[320,128,128]{2,1,0:T(8,128)(2,1)S(1)}, bf16[320,128,128]{2,1,0:T(8,128)(2,1)}, u32[]{:S(2)}) copy-start(bf16[320,128,128]{2,1,0:T(8,128)(2,1)} %get-tuple-element.9.recv_ref) | copy-start | bytes 31457284
  281.3 0.9 copy-start.4

commit v2 on v1

--- a/solution.py
+++ b/solution.py
@@ -11,6 +11,8 @@
 SLOT_DEV = 64
 VSLOT_DEV = 16
 LANES = 128
+DIRECT = 80
+VMEM_LIMIT = 58 * 1024 * 1024
 MESH = pl.DeviceIdType.MESH
 
 
@@ -110,74 +112,213 @@
         drain(lax.rem(live + 1, 2))
 
 
-def exchange_kernel(peers, columns, room, auxrows, send, aux, recv, auxrecv, sems, auxsems, own):
-    me = lax.axis_index("grp") * columns + lax.axis_index("blk")
-
-    def coords(d):
-        return (d // columns, d % columns)
+def exchange_kernel(
+    groups,
+    columns,
+    room,
+    vrows,
+    auxrows,
+    direct,
+    send,
+    aux,
+    recv,
+    relay,
+    auxrecv,
+    auxrelay,
+    sems,
+    auxsems,
+    own,
+):
+    peers = groups * columns
+    part = columns // 2
+    half = peers // 2
+    tile = BLOCK_UNKNOWNS
+    g, c = lax.axis_index("grp"), lax.axis_index("blk")
+    me = g * columns + c
+    base = (c // part) * part
+    inner = c % part
+    mine = g * part + inner
+
+    def near(j):
+        return (g + j // part) % groups, base + (inner + j % part) % part
+
+    def far(j):
+        return (g + j // part) % groups, (part - base) + (inner + j % part) % part
 
     barrier = pltpu.get_barrier_semaphore()
 
     @pl.loop(1, peers)
     def _(k):
+        d = (me + k) % peers
         pl.semaphore_signal(
-            barrier, inc=1, device_id=coords((me + k) % peers), device_id_type=MESH
+            barrier, inc=1, device_id=(d // columns, d % columns), device_id_type=MESH
         )
 
     pl.semaphore_wait(barrier, peers - 1)
 
-    def tile_copy(k):
-        d = (me + k) % peers
+    def remote(src, dst, table, kind, j, device):
         return pltpu.make_async_remote_copy(
-            src_ref=send.at[pl.ds(d * room, room)],
-            dst_ref=recv.at[pl.ds(me * room, room)],
-            send_sem=sems.at[0, k],
-            recv_sem=sems.at[1, k],
-            device_id=coords(d),
+            src_ref=src,
+            dst_ref=dst,
+            send_sem=table.at[2 * kind, j],
+            recv_sem=table.at[2 * kind + 1, j],
+            device_id=device,
             device_id_type=MESH,
         )
 
-    def aux_copy(k):
-        d = (me + k) % peers
-        return pltpu.make_async_remote_copy(
-            src_ref=aux.at[pl.ds(d * auxrows, auxrows)],
-            dst_ref=auxrecv.at[pl.ds(me * auxrows, auxrows)],
-            send_sem=auxsems.at[0, k],
-            recv_sem=auxsems.at[1, k],
-            device_id=coords(d),
-            device_id_type=MESH,
-        )
-
-    @pl.loop(1, peers)
-    def _(k):
-        tile_copy(k).start()
-        aux_copy(k).start()
-
-    mine = pltpu.make_async_copy(
-        send.at[pl.ds(me * room, room)], recv.at[pl.ds(me * room, room)], own.at[0]
+    def flat(device):
+        return device[0] * columns + device[1]
+
+    def near_copies(j):
+        device = near(j)
+        d = flat(device)
+        return (
+            remote(
+                send.at[pl.ds(d * room, room)],
+                recv.at[pl.ds(me * room, room)],
+                sems, 0, j, device,
+            ),
+            remote(
+                aux.at[pl.ds(d * auxrows, auxrows)],
+                auxrecv.at[pl.ds(me * auxrows, auxrows)],
+                auxsems, 0, j, device,
+            ),
+        )
+
+    def far_copies(j):
+        device = far(j)
+        d = flat(device)
+        return (
+            remote(
+                send.at[pl.ds(d * room, room), pl.ds(0, direct)],
+                recv.at[pl.ds(me * room, room), pl.ds(0, direct)],
+                sems, 1, j, device,
+            ),
+            remote(
+                aux.at[pl.ds(d * auxrows, auxrows)],
+                auxrecv.at[pl.ds(me * auxrows, auxrows)],
+                auxsems, 1, j, device,
+            ),
+        )
+
+    def relay_copies(j):
+        device = near(j)
+        d = flat(far(j))
+        return (
+            remote(
+                send.at[pl.ds(d * room, room), pl.ds(direct, tile - direct)],
+                relay.at[pl.ds(mine * room, room)],
+                sems, 2, j, device,
+            ),
+            remote(
+                aux.at[pl.ds(d * auxrows + vrows, 8)],
+                auxrelay.at[pl.ds(mine * 8, 8)],
+                auxsems, 2, j, device,
+            ),
+        )
+
+    for copy in far_copies(0):
+        copy.start()
+
+    @pl.loop(1, half)
+    def _(j):
+        for copy in far_copies(j) + relay_copies(j) + near_copies(j):
+            copy.start()
+
+    twin = flat(far(0))
+    local = (
+        pltpu.make_async_copy(
+            send.at[pl.ds(me * room, room)], recv.at[pl.ds(me * room, room)], own.at[0]
+        ),
+        pltpu.make_async_copy(
+            aux.at[pl.ds(me * auxrows, auxrows)],
+            auxrecv.at[pl.ds(me * auxrows, auxrows)],
+            own.at[1],
+        ),
+        pltpu.make_async_copy(
+            send.at[pl.ds(twin * room, room), pl.ds(direct, tile - direct)],
+            relay.at[pl.ds(mine * room, room)],
+            own.at[2],
+        ),
+        pltpu.make_async_copy(
+            aux.at[pl.ds(twin * auxrows + vrows, 8)], auxrelay.at[pl.ds(mine * 8, 8)], own.at[3]
+        ),
     )
-    auxmine = pltpu.make_async_copy(
-        aux.at[pl.ds(me * auxrows, auxrows)], auxrecv.at[pl.ds(me * auxrows, auxrows)], own.at[1]
+    for copy in local:
+        copy.start()
+    for copy in local:
+        copy.wait()
+    for copy in far_copies(0):
+        copy.wait()
+
+    @pl.loop(1, half)
+    def _(j):
+        for copy in far_copies(j) + relay_copies(j) + near_copies(j):
+            copy.wait()
+
+
+def relay_kernel(group, room, ids, relay_ref, out_ref, total):
+    step = pl.program_id(0)
+
+    @pl.when(step == 0)
+    def _():
+        total[...] = jnp.zeros_like(total)
+
+    @pl.loop(0, group * room)
+    def _(t):
+        target = ids[step * group * room + t]
+
+        @pl.when(target >= 0)
+        def _():
+            total[target] += relay_ref[t].astype(jnp.float32)
+
+    @pl.when(step == pl.num_programs(0) - 1)
+    def _():
+        out_ref[...] = total[...].astype(out_ref.dtype)
+
+
+def swap_kernel(columns, mine, other, sems):
+    part = columns // 2
+    g, c = lax.axis_index("grp"), lax.axis_index("blk")
+    twin = (g, (c + part) % columns)
+    barrier = pltpu.get_barrier_semaphore()
+    pl.semaphore_signal(barrier, inc=1, device_id=twin, device_id_type=MESH)
+    pl.semaphore_wait(barrier, 1)
+    copy = pltpu.make_async_remote_copy(
+        src_ref=mine,
+        dst_ref=other,
+        send_sem=sems.at[0],
+        recv_sem=sems.at[1],
+        device_id=twin,
+        device_id_type=MESH,
     )
-    mine.start()
-    auxmine.start()
-    mine.wait()
-    auxmine.wait()
-
-    @pl.loop(1, peers)
-    def _(k):
-        tile_copy(k).wait()
-        aux_copy(k).wait()
+    copy.start()
+    copy.wait()
 
 
 def sum_kernel(
-    peers, group, room, vroom, auxrows, ids, vids, recv_ref, aux_ref, out_ref, loads_ref
+    peers,
+    group,
+    room,
+    vroom,
+    auxrows,
+    direct,
+    ids,
+    vids,
+    close,
+    recv_ref,
+    aux_ref,
+    far_ref,
+    out_ref,
+    loads_ref,
 ):
     step = pl.program_id(0)
+    tile = BLOCK_UNKNOWNS
 
     @pl.when(step == 0)
     def _():
-        out_ref[...] = jnp.zeros_like(out_ref)
+        out_ref[:, :direct, :] = jnp.zeros((SLOT_DEV, direct, tile), jnp.float32)
+        out_ref[:, direct:, :] = far_ref[...].astype(jnp.float32)
         loads_ref[...] = jnp.zeros_like(loads_ref)
 
         @pl.loop(0, peers)
@@ -189,13 +330,21 @@
                 def _():
                     loads_ref[pl.ds(target, 1), :] += aux_ref[pl.ds(p * auxrows + v, 1), :]
 
-    @pl.loop(0, group * room)
-    def _(t):
-        target = ids[step * group * room + t]
-
-        @pl.when(target >= 0)
-        def _():
-            out_ref[target] += recv_ref[t].astype(jnp.float32)
+    for p in range(group):
+        whole = close[step * group + p] > 0
+
+        @pl.loop(0, room)
+        def _(r):
+            t = p * room + r
+            target = ids[step * group * room + t]
+
+            @pl.when((target >= 0) & whole)
+            def _():
+                out_ref[target] += recv_ref[t].astype(jnp.float32)
+
+            @pl.when((target >= 0) & jnp.logical_not(whole))
+            def _():
+                out_ref[target, :direct, :] += recv_ref[t, :direct, :].astype(jnp.float32)
 
 
 def shards(
@@ -270,41 +419,83 @@
             jax.ShapeDtypeStruct((peers * auxrows, LANES), jnp.float32),
         ],
         compiler_params=pltpu.CompilerParams(
-            dimension_semantics=("arbitrary",), vmem_limit_bytes=40 * 1024 * 1024
+            dimension_semantics=("arbitrary",), vmem_limit_bytes=VMEM_LIMIT
         ),
         name="condense",
     )(counts, pos, vpos, inv_factor, coupling, boundary, load_int, load_bnd, table)
 
-    recv, auxrecv = pl.pallas_call(
-        functools.partial(exchange_kernel, peers, columns, room, auxrows),
+    half = peers // 2
+    recv, relay, auxrecv, auxrelay = pl.pallas_call(
+        functools.partial(
+            exchange_kernel, peers // columns, columns, room, vrows, auxrows, DIRECT
+        ),
         in_specs=[pl.BlockSpec(memory_space=pl.ANY)] * 2,
-        out_specs=[pl.BlockSpec(memory_space=pl.ANY)] * 2,
+        out_specs=[pl.BlockSpec(memory_space=pl.ANY)] * 4,
         out_shape=[
             jax.ShapeDtypeStruct((peers * room, tile, tile), jnp.bfloat16),
+            jax.ShapeDtypeStruct((half * room, tile - DIRECT, tile), jnp.bfloat16),
             jax.ShapeDtypeStruct((peers * auxrows, LANES), jnp.float32),
+            jax.ShapeDtypeStruct((half * 8, LANES), jnp.float32),
         ],
         scratch_shapes=[
-            pltpu.SemaphoreType.DMA((2, peers)),
-            pltpu.SemaphoreType.DMA((2, peers)),
-            pltpu.SemaphoreType.DMA((2,)),
+            pltpu.SemaphoreType.DMA((6, half)),
+            pltpu.SemaphoreType.DMA((6, half)),
+            pltpu.SemaphoreType.DMA((4,)),
         ],
-        compiler_params=pltpu.CompilerParams(collective_id=0, has_side_effects=True),
+        compiler_params=pltpu.CompilerParams(
+            collective_id=0, has_side_effects=True, vmem_limit_bytes=VMEM_LIMIT
+        ),
         name="exchange",
     )(send, aux)
+
+    relay_ids = auxrelay.reshape(half, 8, LANES)[:, 0, :room].astype(jnp.int32).reshape(-1)
+    group = 4 if half % 4 == 0 else 1
+    partial = pl.pallas_call(
+        functools.partial(relay_kernel, group, room),
+        grid_spec=pltpu.PrefetchScalarGridSpec(
+            num_scalar_prefetch=1,
+            grid=(half // group,),
+            in_specs=[
+                pl.BlockSpec((group * room, tile - DIRECT, tile), lambda s, *_: (s, 0, 0)),
+            ],
+            out_specs=pl.BlockSpec((SLOT_DEV, tile - DIRECT, tile), lambda s, *_: (0, 0, 0)),
+            scratch_shapes=[pltpu.VMEM((SLOT_DEV, tile - DIRECT, tile), jnp.float32)],
+        ),
+        out_shape=jax.ShapeDtypeStruct((SLOT_DEV, tile - DIRECT, tile), jnp.bfloat16),
+        compiler_params=pltpu.CompilerParams(
+            dimension_semantics=("arbitrary",), vmem_limit_bytes=VMEM_LIMIT
+        ),
+        name="relay",
+    )(relay_ids, relay)
+
+    other = pl.pallas_call(
+        functools.partial(swap_kernel, columns),
+        in_specs=[pl.BlockSpec(memory_space=pl.ANY)],
+        out_specs=pl.BlockSpec(memory_space=pl.ANY),
+        out_shape=jax.ShapeDtypeStruct(partial.shape, jnp.bfloat16),
+        scratch_shapes=[pltpu.SemaphoreType.DMA((2,))],
+        compiler_params=pltpu.CompilerParams(
+            collective_id=1, has_side_effects=True, vmem_limit_bytes=VMEM_LIMIT
+        ),
+        name="swap",
+    )(partial)
 
     got = auxrecv.reshape(peers, auxrows, LANES)
     got_ids = got[:, vrows, :room].astype(jnp.int32).reshape(-1)
     got_vids = got[:, vrows + 1, :vroom].astype(jnp.int32).reshape(-1)
-    group = 4 if peers % 4 == 0 else 1
+    part = columns // 2
+    source = jnp.arange(peers, dtype=jnp.int32) % columns
+    close = (source // part == lax.axis_index("blk") // part).astype(jnp.int32)
 
     assembled, loads = pl.pallas_call(
-        functools.partial(sum_kernel, peers, group, room, vroom, auxrows),
+        functools.partial(sum_kernel, peers, group, room, vroom, auxrows, DIRECT),
         grid_spec=pltpu.PrefetchScalarGridSpec(
-            num_scalar_prefetch=2,
+            num_scalar_prefetch=3,
             grid=(peers // group,),
             in_specs=[
                 pl.BlockSpec((group * room, tile, tile), lambda s, *_: (s, 0, 0)),
                 pl.BlockSpec((peers * auxrows, LANES), whole),
+                pl.BlockSpec((SLOT_DEV, tile - DIRECT, tile), lambda s, *_: (0, 0, 0)),
             ],
             out_specs=[
                 pl.BlockSpec((SLOT_DEV, tile, tile), lambda s, *_: (0, 0, 0)),
@@ -316,10 +507,10 @@
             jax.ShapeDtypeStruct((VSLOT_DEV, LANES), jnp.float32),
         ],
         compiler_params=pltpu.CompilerParams(
-            dimension_semantics=("arbitrary",), vmem_limit_bytes=40 * 1024 * 1024
+            dimension_semantics=("arbitrary",), vmem_limit_bytes=VMEM_LIMIT
         ),
         name="assemble",
-    )(got_ids, got_vids, recv, auxrecv)
+    )(got_ids, got_vids, close, recv, auxrecv, other)
     return (assembled, loads)
 
 

time: 292 us -> 259 us (0.89); the launches traced: 291 us -> 254 us
  Pallas kernels: 268 us -> 240 us
  local copies, waits for them, and re-layouts: 17.4 us -> 6.59 us
    pallas_call x1 -> x3, Pallas kernels: 247 us -> 213 us  [the longest x1 174 us: shards(): pl.pallas_call(functools.partial(exchange_kernel, peers // columns, colum...]
    unnamed x16 -> x0, local copies, waits for them, and re-layouts: 13.5 us -> none
    pallas_call x1, Pallas kernels: 9.03 us -> 14 us  [shards(): pl.pallas_call(functools.partial(sum_kernel, peers, group, room, vroom, a...]
where the time goes in v2:
time: 259 us; the launch traced here: 254 us
  Pallas kernels  240 us (93%)
  local copies, waits for them, and re-layouts  6.59 us (3%)
  other arithmetic  6.36 us (2%)
    pallas_call x1, Pallas kernels, shards(): pl.pallas_call(functools.partial(exchange_kernel, peers // columns, colum...  174 us
    pallas_call x1, Pallas kernels, shards(): pl.pallas_call(functools.partial(swap_kernel, columns), in_specs=[pl.Bloc...  33.4 us
    pallas_call x1, Pallas kernels, shards(): pl.pallas_call(functools.partial(sum_kernel, peers, group, room, vroom, a...  14 us
    pallas_call x1, Pallas kernels, shards(): pl.pallas_call(functools.partial(condense_kernel, emax, tiles), grid_spec...  13 us
    pallas_call x1, Pallas kernels, shards(): pl.pallas_call(functools.partial(relay_kernel, group, room), grid_spec=pl...  5.84 us

profile of v2, /device:TPU:11, one launch (start us, length us, event | category | flops | bytes accessed | tf_op | source)
XLA Modules:
  0.0 254.3 jit_solution(8365984012109524940)
XLA Ops:
  0.6 0.7 reduce
  1.3 0.1 reshape.158
  1.4 0.2 convert_reduce_fusion
  1.6 0.1 iota_compare_fusion.1
  2.4 0.8 broadcast_in_dim.93
  3.2 1.4 select_reduce_fusion
  4.6 0.7 reduce.1
  5.3 0.1 reshape.159
  5.4 0.2 convert_reduce_fusion.1
  5.5 0.1 iota_compare_fusion.3
  5.6 0.1 iota_compare_fusion.4
  5.7 0.8 broadcast_in_dim.101
  6.5 0.3 select_reduce_fusion.1
  6.8 0.1 broadcast_in_dim.91
  6.9 0.1 broadcast_in_dim.99
  7.0 0.9 fusion.1.ids_ref
  7.9 0.5 multiply_add_fusion.1.vpos
  8.5 0.6 multiply_add_fusion.pos
  9.0 13.0 %condense.1 = (bf16[320,128,128]{2,1,0:T(8,128)(2,1)}, f32[512,128]{1,0:T(8,128)}) custom-call(s32[1]{0:T(128)S(6)} %copy.22.counts, s32[216]{0:T(256)} %multiply_add_fusion.pos, s32[36]{0:T(128)} %multiply_add_fusion.1.vpos, bf16[6,384,384]{2,1,0:T(8,128)(2,1)} %factor_ref.1, bf16[6,384,768]{2,1,0:T(8,128)(2,1)} %couple_ref.1, ...), custom_call_target="tpu_custom_call" | custom-call | tf_op jit(solution)/shard_map/condense/pallas_call | solution.py:395
  22.0 173.7 %exchange.1 = (bf16[320,128,128]{2,1,0:T(8,128)(2,1)}, bf16[160,48,128]{2,1,0:T(8,128)(2,1)}, f32[512,128]{1,0:T(8,128)}, f32[128,128]{1,0:T(8,128)}) custom-call(bf16[320,128,128]{2,1,0:T(8,128)(2,1)} %get-tuple-element.8.send, f32[512,128]{1,0:T(8,128)} %get-tuple-element.9.aux), custom_call_target="tpu_custom_call" | custom-call | tf_op jit(solution)/shard_map/exchange/pallas_call | solution.py:428
  195.8 0.8 slice.14
  196.6 0.7 convert_element_type.43.ids
  197.3 5.8 %relay.1.mine = bf16[64,48,128]{2,1,0:T(8,128)(2,1)} custom-call(s32[160]{0:T(256)} %convert_element_type.43.ids, bf16[160,48,128]{2,1,0:T(8,128)(2,1)} %get-tuple-element.13.relay_ref), custom_call_target="tpu_custom_call" | custom-call | tf_op jit(solution)/shard_map/relay/pallas_call | solution.py:453
  203.1 33.4 %swap.1.far_ref = bf16[64,48,128]{2,1,0:T(8,128)(2,1)} custom-call(bf16[64,48,128]{2,1,0:T(8,128)(2,1)} %relay.1.mine), custom_call_target="tpu_custom_call" | custom-call | tf_op jit(solution)/shard_map/swap/pallas_call | solution.py:471
  236.5 0.5 compare_convert_fusion.close
  237.1 0.9 slice.12
  238.0 0.7 convert_element_type.38.ids
  238.7 0.9 slice.13
  239.6 0.7 convert_element_type.40.vids
  240.3 14.0 %assemble.1 = (f32[64,128,128]{2,1,0:T(8,128)}, f32[16,128]{1,0:T(8,128)}) custom-call(s32[320]{0:T(512)} %convert_element_type.38.ids, s32[64]{0:T(128)} %convert_element_type.40.vids, s32[32]{0:T(128)} %compare_convert_fusion.close, bf16[320,128,128]{2,1,0:T(8,128)(2,1)} %get-tuple-element.11.recv_ref, f32[512,128]{1,0:T(8,128)} %get-tuple-element.10.aux_ref, ...), custom_call_target="tpu_custom_call" | custom-call | tf_op jit(solution)/shard_map/assemble/pallas_call | solution.py:490
  (10 shorter events, 0.1 us)

commit v3 on v2

--- a/solution.py
+++ b/solution.py
@@ -264,87 +264,68 @@
     def _():
         total[...] = jnp.zeros_like(total)
 
-    @pl.loop(0, group * room)
-    def _(t):
-        target = ids[step * group * room + t]
-
-        @pl.when(target >= 0)
-        def _():
-            total[target] += relay_ref[t].astype(jnp.float32)
+    for p in range(group):
+
+        @pl.loop(0, room)
+        def _(r):
+            target = ids[p * 8, r].astype(jnp.int32)
+
+            @pl.when(target >= 0)
+            def _():
+                total[target] += relay_ref[p * room + r].astype(jnp.float32)
 
     @pl.when(step == pl.num_programs(0) - 1)
     def _():
         out_ref[...] = total[...].astype(out_ref.dtype)
 
 
-def swap_kernel(columns, mine, other, sems):
-    part = columns // 2
-    g, c = lax.axis_index("grp"), lax.axis_index("blk")
-    twin = (g, (c + part) % columns)
-    barrier = pltpu.get_barrier_semaphore()
-    pl.semaphore_signal(barrier, inc=1, device_id=twin, device_id_type=MESH)
-    pl.semaphore_wait(barrier, 1)
-    copy = pltpu.make_async_remote_copy(
-        src_ref=mine,
-        dst_ref=other,
-        send_sem=sems.at[0],
-        recv_sem=sems.at[1],
-        device_id=twin,
-        device_id_type=MESH,
-    )
-    copy.start()
-    copy.wait()
-
-
 def sum_kernel(
-    peers,
-    group,
-    room,
-    vroom,
-    auxrows,
-    direct,
-    ids,
-    vids,
-    close,
-    recv_ref,
-    aux_ref,
-    far_ref,
-    out_ref,
-    loads_ref,
+    group, room, vroom, vrows, direct, close, ids, recv_ref, aux_ref, out_ref, loads_ref
 ):
     step = pl.program_id(0)
-    tile = BLOCK_UNKNOWNS
+    auxrows = vrows + 8
 
     @pl.when(step == 0)
     def _():
-        out_ref[:, :direct, :] = jnp.zeros((SLOT_DEV, direct, tile), jnp.float32)
-        out_ref[:, direct:, :] = far_ref[...].astype(jnp.float32)
+        out_ref[...] = jnp.zeros_like(out_ref)
         loads_ref[...] = jnp.zeros_like(loads_ref)
 
-        @pl.loop(0, peers)
-        def _(p):
-            for v in range(vroom):
-                target = vids[p * vroom + v]
+    for p in range(group):
+        first = p * auxrows
+        whole = close[step * group + p] > 0
+
+        for v in range(vroom):
+            slot = ids[first + vrows + 1, v].astype(jnp.int32)
+
+            @pl.when(slot >= 0)
+            def _():
+                loads_ref[pl.ds(slot, 1), :] += aux_ref[pl.ds(first + v, 1), :]
+
+        @pl.when(whole)
+        def _():
+            @pl.loop(0, room)
+            def _(r):
+                target = ids[first + vrows, r].astype(jnp.int32)
 
                 @pl.when(target >= 0)
                 def _():
-                    loads_ref[pl.ds(target, 1), :] += aux_ref[pl.ds(p * auxrows + v, 1), :]
-
-    for p in range(group):
-        whole = close[step * group + p] > 0
-
-        @pl.loop(0, room)
-        def _(r):
-            t = p * room + r
-            target = ids[step * group * room + t]
-
-            @pl.when((target >= 0) & whole)
-            def _():
-                out_ref[target] += recv_ref[t].astype(jnp.float32)
-
-            @pl.when((target >= 0) & jnp.logical_not(whole))
-            def _():
-                out_ref[target, :direct, :] += recv_ref[t, :direct, :].astype(jnp.float32)
+                    out_ref[target] += recv_ref[p * room + r].astype(jnp.float32)
+
+        @pl.when(jnp.logical_not(whole))
+        def _():
+            @pl.loop(0, room)
+            def _(r):
+                target = ids[first + vrows, r].astype(jnp.int32)
+
+                @pl.when(target >= 0)
+                def _():
+                    out_ref[target, :direct, :] += recv_ref[p * room + r, :direct, :].astype(
+                        jnp.float32
+                    )
+
+
+def add_kernel(sum_ref, far_ref, out_ref):
+    out_ref[...] = sum_ref[...] + far_ref[...].astype(jnp.float32)
 
 
 def shards(
@@ -448,54 +429,40 @@
         name="exchange",
     )(send, aux)
 
-    relay_ids = auxrelay.reshape(half, 8, LANES)[:, 0, :room].astype(jnp.int32).reshape(-1)
     group = 4 if half % 4 == 0 else 1
+    rest = tile - DIRECT
     partial = pl.pallas_call(
         functools.partial(relay_kernel, group, room),
+        grid=(half // group,),
+        in_specs=[
+            pl.BlockSpec((group * 8, LANES), lambda s: (s, 0), memory_space=pltpu.SMEM),
+            pl.BlockSpec((group * room, rest, tile), lambda s: (s, 0, 0)),
+        ],
+        out_specs=pl.BlockSpec((SLOT_DEV, rest, tile), lambda s: (0, 0, 0)),
+        scratch_shapes=[pltpu.VMEM((SLOT_DEV, rest, tile), jnp.float32)],
+        out_shape=jax.ShapeDtypeStruct((SLOT_DEV, rest, tile), jnp.bfloat16),
+        compiler_params=pltpu.CompilerParams(
+            dimension_semantics=("arbitrary",), vmem_limit_bytes=VMEM_LIMIT
+        ),
+        name="relay",
+    )(auxrelay, relay)
+
+    part = columns // 2
+    other = lax.ppermute(partial, "blk", [(c, (c + part) % columns) for c in range(columns)])
+
+    source = jnp.arange(peers, dtype=jnp.int32) % columns
+    close = (source // part == lax.axis_index("blk") // part).astype(jnp.int32)
+    summed, loads = pl.pallas_call(
+        functools.partial(sum_kernel, group, room, vroom, vrows, DIRECT),
         grid_spec=pltpu.PrefetchScalarGridSpec(
             num_scalar_prefetch=1,
-            grid=(half // group,),
-            in_specs=[
-                pl.BlockSpec((group * room, tile - DIRECT, tile), lambda s, *_: (s, 0, 0)),
-            ],
-            out_specs=pl.BlockSpec((SLOT_DEV, tile - DIRECT, tile), lambda s, *_: (0, 0, 0)),
-            scratch_shapes=[pltpu.VMEM((SLOT_DEV, tile - DIRECT, tile), jnp.float32)],
-        ),
-        out_shape=jax.ShapeDtypeStruct((SLOT_DEV, tile - DIRECT, tile), jnp.bfloat16),
-        compiler_params=pltpu.CompilerParams(
-            dimension_semantics=("arbitrary",), vmem_limit_bytes=VMEM_LIMIT
-        ),
-        name="relay",
-    )(relay_ids, relay)
-
-    other = pl.pallas_call(
-        functools.partial(swap_kernel, columns),
-        in_specs=[pl.BlockSpec(memory_space=pl.ANY)],
-        out_specs=pl.BlockSpec(memory_space=pl.ANY),
-        out_shape=jax.ShapeDtypeStruct(partial.shape, jnp.bfloat16),
-        scratch_shapes=[pltpu.SemaphoreType.DMA((2,))],
-        compiler_params=pltpu.CompilerParams(
-            collective_id=1, has_side_effects=True, vmem_limit_bytes=VMEM_LIMIT
-        ),
-        name="swap",
-    )(partial)
-
-    got = auxrecv.reshape(peers, auxrows, LANES)
-    got_ids = got[:, vrows, :room].astype(jnp.int32).reshape(-1)
-    got_vids = got[:, vrows + 1, :vroom].astype(jnp.int32).reshape(-1)
-    part = columns // 2
-    source = jnp.arange(peers, dtype=jnp.int32) % columns
-    close = (source // part == lax.axis_index("blk") // part).astype(jnp.int32)
-
-    assembled, loads = pl.pallas_call(
-        functools.partial(sum_kernel, peers, group, room, vroom, auxrows, DIRECT),
-        grid_spec=pltpu.PrefetchScalarGridSpec(
-            num_scalar_prefetch=3,
             grid=(peers // group,),
             in_specs=[
+                pl.BlockSpec(
+                    (group * auxrows, LANES), lambda s, *_: (s, 0), memory_space=pltpu.SMEM
+                ),
                 pl.BlockSpec((group * room, tile, tile), lambda s, *_: (s, 0, 0)),
-                pl.BlockSpec((peers * auxrows, LANES), whole),
-                pl.BlockSpec((SLOT_DEV, tile - DIRECT, tile), lambda s, *_: (0, 0, 0)),
+                pl.BlockSpec((group * auxrows, LANES), lambda s, *_: (s, 0)),
             ],
             out_specs=[
                 pl.BlockSpec((SLOT_DEV, tile, tile), lambda s, *_: (0, 0, 0)),
@@ -509,8 +476,28 @@
         compiler_params=pltpu.CompilerParams(
             dimension_semantics=("arbitrary",), vmem_limit_bytes=VMEM_LIMIT
         ),
+        cost_estimate=pl.CostEstimate(
+            flops=peers * room * tile * tile, bytes_accessed=30_000_000, transcendentals=0
+        ),
         name="assemble",
-    )(got_ids, got_vids, close, recv, auxrecv, other)
+    )(close, auxrecv, recv, auxrecv)
+
+    strip = 16
+    assembled = pl.pallas_call(
+        add_kernel,
+        grid=(rest // strip,),
+        in_specs=[
+            pl.BlockSpec((SLOT_DEV, strip, tile), lambda s: (0, DIRECT // strip + s, 0)),
+            pl.BlockSpec((SLOT_DEV, strip, tile), lambda s: (0, s, 0)),
+        ],
+        out_specs=pl.BlockSpec((SLOT_DEV, strip, tile), lambda s: (0, DIRECT // strip + s, 0)),
+        out_shape=jax.ShapeDtypeStruct((SLOT_DEV, tile, tile), jnp.float32),
+        input_output_aliases={0: 0},
+        compiler_params=pltpu.CompilerParams(
+            dimension_semantics=("arbitrary",), vmem_limit_bytes=VMEM_LIMIT
+        ),
+        name="add_partial",
+    )(summed, other)
     return (assembled, loads)
 
 

time: 259 us -> 244 us (0.942)
  Pallas kernels: 240 us -> 210 us
  waiting for transfers between devices: 0 us -> 20.1 us
  local copies, waits for them, and re-layouts: 6.59 us -> 2.76 us
    pallas_call x3, Pallas kernels: 53.3 us -> 22.2 us  [the longest x1 13 us: shards(): pl.pallas_call(functools.partial(sum_kernel, group, room, vroom, vrows, D...]
    ppermute x0 -> x1, waiting for transfers between devices: none -> 20.1 us  [shards(): lax.ppermute(partial, 'blk', [(c, (c + part) % columns) for c in range(co...]
    slice x3 -> x0, local copies, waits for them, and re-layouts: 2.68 us -> none  [the longest x1 0.92 us: shards(): got_vids = got[:, vrows + 1, :vroom].astype(jnp.int32).reshape(-1)]
  transfers between devices with their start and end apart: 0 -> 1, of which waited for: 0 -> 1; matrix products, arithmetic and copies ran while one was open for 0% -> 0% of each run, Pallas kernels for 0% -> 5%
where the time goes in v3:
time: 244 us; the launch traced here: 240 us
  Pallas kernels  210 us (86%)
  waiting for transfers between devices  20.1 us (8%)
  other arithmetic  6.34 us (3%)
  local copies, waits for them, and re-layouts  2.76 us (1%)
    pallas_call x1, Pallas kernels, shards(): pl.pallas_call(functools.partial(exchange_kernel, peers // columns, colum...  173 us
    ppermute x1, waiting for transfers between devices, shards(): lax.ppermute(partial, 'blk', [(c, (c + part) % columns) for c in range(co...  20.1 us
    pallas_call x1, Pallas kernels, shards(): pl.pallas_call(functools.partial(condense_kernel, emax, tiles), grid_spec...  14.6 us
    pallas_call x1, Pallas kernels, shards(): pl.pallas_call(functools.partial(sum_kernel, group, room, vroom, vrows, D...  13 us
    pallas_call x1, Pallas kernels, shards(): pl.pallas_call(functools.partial(relay_kernel, group, room), grid=(half /...  5.6 us
  transfers between devices with their start and end apart: 1, of which 1 were waited for; matrix products, arithmetic and copies ran while one was open for 0% of the time, Pallas kernels for 5%

profile of v3, /device:TPU:11, one launch (start us, length us, event | category | flops | bytes accessed | tf_op | source)
XLA Modules:
  0.0 240.2 jit_solution(4474536103016940917)
XLA Ops:
  0.6 0.7 reduce
  1.3 0.1 reshape.143
  1.4 0.2 convert_reduce_fusion
  1.6 0.7 reduce.1
  2.3 0.1 reshape.144
  2.4 0.2 convert_reduce_fusion.1
  2.6 0.1 iota_compare_fusion.4
  2.7 0.1 iota_compare_fusion.1
  2.8 0.6 multiply_add_fusion.pos
  3.4 0.1 iota_compare_fusion.3
  3.4 0.5 multiply_add_fusion.1.vpos
  4.6 0.8 broadcast_in_dim.93
  5.4 0.8 broadcast_in_dim.101
  6.2 0.1 broadcast_in_dim.91
  6.3 0.1 broadcast_in_dim.99
  6.4 1.4 select_reduce_fusion
  7.8 0.3 select_reduce_fusion.1
  8.1 0.9 fusion.1.ids_ref
  9.0 14.6 %condense.1 = (bf16[320,128,128]{2,1,0:T(8,128)(2,1)}, f32[512,128]{1,0:T(8,128)}) custom-call(s32[1]{0:T(128)S(6)} %copy.14.counts, s32[216]{0:T(256)} %multiply_add_fusion.pos, s32[36]{0:T(128)} %multiply_add_fusion.1.vpos, bf16[6,384,384]{2,1,0:T(8,128)(2,1)} %factor_ref.1, bf16[6,384,768]{2,1,0:T(8,128)(2,1)} %couple_ref.1, ...), custom_call_target="tpu_custom_call" | custom-call | tf_op jit(solution)/shard_map/condense/pallas_call | solution.py:376
  23.7 172.8 %exchange.1 = (bf16[320,128,128]{2,1,0:T(8,128)(2,1)}, bf16[160,48,128]{2,1,0:T(8,128)(2,1)}, f32[512,128]{1,0:T(8,128)}, f32[128,128]{1,0:T(8,128)}) custom-call(bf16[320,128,128]{2,1,0:T(8,128)(2,1)} %get-tuple-element.10.send, f32[512,128]{1,0:T(8,128)} %get-tuple-element.11.aux), custom_call_target="tpu_custom_call" | custom-call | tf_op jit(solution)/shard_map/exchange/pallas_call | solution.py:409
  196.4 5.6 %relay.1 = bf16[64,48,128]{2,1,0:T(8,128)(2,1)} custom-call(f32[128,128]{1,0:T(8,128)} %get-tuple-element.15.ids, bf16[160,48,128]{2,1,0:T(8,128)(2,1)} %get-tuple-element.16.relay_ref), custom_call_target="tpu_custom_call" | custom-call | tf_op jit(solution)/shard_map/relay/pallas_call | solution.py:434
  202.0 0.0 collective-permute-start
  202.0 0.5 compare_convert_fusion.close
  202.6 13.0 %assemble.1 = (f32[64,128,128]{2,1,0:T(8,128)}, f32[16,128]{1,0:T(8,128)}) custom-call(s32[32]{0:T(128)} %compare_convert_fusion.close, f32[512,128]{1,0:T(8,128)} %get-tuple-element.12.ids.aux_ref, bf16[320,128,128]{2,1,0:T(8,128)(2,1)} %get-tuple-element.13.recv_ref, f32[512,128]{1,0:T(8,128)} %get-tuple-element.12.ids.aux_ref), custom_call_target="tpu_custom_call" | custom-call | flops 5242880 | bytes 30000000 | tf_op jit(solution)/shard_map/assemble/pallas_call | solution.py:455
  215.6 20.1 %collective-permute-done.far_ref = bf16[64,48,128]{2,1,0:T(8,128)(2,1)S(1)} collective-permute-done((bf16[64,48,128]{2,1,0:T(8,128)(2,1)}, bf16[64,48,128]{2,1,0:T(8,128)(2,1)S(1)}, u32[]{:S(2)}, u32[]{:S(2)}) %collective-permute-start) | collective-permute-done | bytes 786464 | tf_op jit(solution)/shard_map/ppermute | solution.py:451
  235.7 0.0 copy-start
  235.7 0.9 copy-done
  236.6 3.6 %add_partial.1 = f32[64,128,128]{2,1,0:T(8,128)} custom-call(f32[64,128,128]{2,1,0:T(8,128)} %get-tuple-element.14.sum_ref, bf16[64,48,128]{2,1,0:T(8,128)(2,1)} %copy-done), custom_call_target="tpu_custom_call", output_to_operand_aliasing={{}: (0, {})} | custom-call | tf_op jit(solution)/shard_map/add_partial/pallas_call | solution.py:486
  (7 shorter events, 0.1 us)
Async XLA Ops:
  202.0 33.7 %collective-permute-start = (bf16[64,48,128]{2,1,0:T(8,128)(2,1)}, bf16[64,48,128]{2,1,0:T(8,128)(2,1)S(1)}, u32[]{:S(2)}, u32[]{:S(2)}) collective-permute-start(bf16[64,48,128]{2,1,0:T(8,128)(2,1)} %relay.1), channel_id=1, source_target_pairs={{0,4},{1,5},{2,6},{3,7},{4,0},{5,1},{6,2},{7,3},{8,12},{9,13},{10,... | collective-permute-start | bytes 2359304 | tf_op jit(solution)/shard_map/ppermute | solution.py:451
  235.7 0.9 copy-start

commit v4 on v3

--- a/solution.py
+++ b/solution.py
@@ -11,7 +11,7 @@
 SLOT_DEV = 64
 VSLOT_DEV = 16
 LANES = 128
-DIRECT = 80
+DIRECT = 64
 VMEM_LIMIT = 58 * 1024 * 1024
 MESH = pl.DeviceIdType.MESH
 
@@ -217,13 +217,22 @@
             ),
         )
 
-    for copy in far_copies(0):
-        copy.start()
-
-    @pl.loop(1, half)
+    @pl.loop(0, half)
     def _(j):
-        for copy in far_copies(j) + relay_copies(j) + near_copies(j):
+        for copy in far_copies(j):
             copy.start()
+        r = (j + half // 3) % half
+        n = (j + 2 * half // 3) % half
+
+        @pl.when(r > 0)
+        def _():
+            for copy in relay_copies(r):
+                copy.start()
+
+        @pl.when(n > 0)
+        def _():
+            for copy in near_copies(n):
+                copy.start()
 
     twin = flat(far(0))
     local = (

time: 244 us -> 247 us (1.012)
  Pallas kernels: 210 us -> 197 us
  waiting for transfers between devices: 20.1 us -> 30.5 us
  starting transfers between devices: 0.01 us -> 4.75 us
    ppermute x1, waiting for transfers between devices: 20.1 us -> 30.5 us  [shards(): lax.ppermute(partial, 'blk', [(c, (c + part) % columns) for c in range(co...]
    pallas_call x1, Pallas kernels: 14.6 us -> 7.92 us  [shards(): pl.pallas_call(functools.partial(condense_kernel, emax, tiles), grid_spec...]
    pallas_call x1, Pallas kernels: 173 us -> 166 us  [shards(): pl.pallas_call(functools.partial(exchange_kernel, peers // columns, colum...]
    ppermute x1, starting transfers between devices: 0.01 us -> 4.75 us  [shards(): lax.ppermute(partial, 'blk', [(c, (c + part) % columns) for c in range(co...]
where the time goes in v4:
time: 247 us; the launch traced here: 243 us
  Pallas kernels  197 us (80%)
  waiting for transfers between devices  30.5 us (12%)
  other arithmetic  6.35 us (3%)
  starting transfers between devices  4.75 us (2%)
  local copies, waits for them, and re-layouts  2.87 us (1%)
    pallas_call x1, Pallas kernels, shards(): pl.pallas_call(functools.partial(exchange_kernel, peers // columns, colum...  166 us
    ppermute x1, waiting for transfers between devices, shards(): lax.ppermute(partial, 'blk', [(c, (c + part) % columns) for c in range(co...  30.5 us
    pallas_call x1, Pallas kernels, shards(): pl.pallas_call(functools.partial(sum_kernel, group, room, vroom, vrows, D...  13 us
    pallas_call x1, Pallas kernels, shards(): pl.pallas_call(functools.partial(condense_kernel, emax, tiles), grid_spec...  7.92 us
    pallas_call x1, Pallas kernels, shards(): pl.pallas_call(functools.partial(relay_kernel, group, room), grid=(half /...  5.81 us
  transfers between devices with their start and end apart: 1, of which 1 were waited for; matrix products, arithmetic and copies ran while one was open for 0% of the time, Pallas kernels for 5%

profile of v4, /device:TPU:11, one launch (start us, length us, event | category | flops | bytes accessed | tf_op | source)
XLA Modules:
  0.0 243.0 jit_solution(12958277218038605669)
XLA Ops:
  0.6 0.7 reduce
  1.3 0.1 reshape.143
  1.4 0.2 convert_reduce_fusion
  1.6 0.7 reduce.1
  2.3 0.1 reshape.144
  2.4 0.2 convert_reduce_fusion.1
  2.6 0.1 iota_compare_fusion.4
  2.7 0.1 iota_compare_fusion.1
  2.8 0.6 multiply_add_fusion.pos
  3.4 0.1 iota_compare_fusion.3
  3.4 0.5 multiply_add_fusion.1.vpos
  4.6 0.8 broadcast_in_dim.93
  5.4 0.8 broadcast_in_dim.101
  6.2 0.1 broadcast_in_dim.91
  6.3 0.1 broadcast_in_dim.99
  6.4 1.4 select_reduce_fusion
  7.8 0.3 select_reduce_fusion.1
  8.1 0.9 fusion.1.ids_ref
  9.0 7.9 %condense.1 = (bf16[320,128,128]{2,1,0:T(8,128)(2,1)}, f32[512,128]{1,0:T(8,128)}) custom-call(s32[1]{0:T(128)S(6)} %copy.14.counts, s32[216]{0:T(256)} %multiply_add_fusion.pos, s32[36]{0:T(128)} %multiply_add_fusion.1.vpos, bf16[6,384,384]{2,1,0:T(8,128)(2,1)} %factor_ref.1, bf16[6,384,768]{2,1,0:T(8,128)(2,1)} %couple_ref.1, ...), custom_call_target="tpu_custom_call" | custom-call | tf_op jit(solution)/shard_map/condense/pallas_call | solution.py:385
  17.0 166.4 %exchange.1 = (bf16[320,128,128]{2,1,0:T(8,128)(2,1)}, bf16[160,64,128]{2,1,0:T(8,128)(2,1)}, f32[512,128]{1,0:T(8,128)}, f32[128,128]{1,0:T(8,128)}) custom-call(bf16[320,128,128]{2,1,0:T(8,128)(2,1)} %get-tuple-element.10.send, f32[512,128]{1,0:T(8,128)} %get-tuple-element.11.aux), custom_call_target="tpu_custom_call" | custom-call | tf_op jit(solution)/shard_map/exchange/pallas_call | solution.py:418
  183.4 5.8 %relay.1 = bf16[64,64,128]{2,1,0:T(8,128)(2,1)} custom-call(f32[128,128]{1,0:T(8,128)} %get-tuple-element.15.ids, bf16[160,64,128]{2,1,0:T(8,128)(2,1)} %get-tuple-element.16.relay_ref), custom_call_target="tpu_custom_call" | custom-call | tf_op jit(solution)/shard_map/relay/pallas_call | solution.py:443
  189.2 4.8 %collective-permute-start = (bf16[64,64,128]{2,1,0:T(8,128)(2,1)}, bf16[64,64,128]{2,1,0:T(8,128)(2,1)S(1)}, u32[]{:S(2)}, u32[]{:S(2)}) collective-permute-start(bf16[64,64,128]{2,1,0:T(8,128)(2,1)} %relay.1), channel_id=1, source_target_pairs={{0,4},{1,5},{2,6},{3,7},{4,0},{5,1},{6,2},{7,3},{8,12},{9,13},{10,... | collective-permute-start | bytes 3145736 | tf_op jit(solution)/shard_map/ppermute | solution.py:460
  193.9 0.5 compare_convert_fusion.close
  194.5 13.0 %assemble.1 = (f32[64,128,128]{2,1,0:T(8,128)}, f32[16,128]{1,0:T(8,128)}) custom-call(s32[32]{0:T(128)} %compare_convert_fusion.close, f32[512,128]{1,0:T(8,128)} %get-tuple-element.12.ids.aux_ref, bf16[320,128,128]{2,1,0:T(8,128)(2,1)} %get-tuple-element.13.recv_ref, f32[512,128]{1,0:T(8,128)} %get-tuple-element.12.ids.aux_ref), custom_call_target="tpu_custom_call" | custom-call | flops 5242880 | bytes 30000000 | tf_op jit(solution)/shard_map/assemble/pallas_call | solution.py:464
  207.5 30.5 %collective-permute-done.far_ref = bf16[64,64,128]{2,1,0:T(8,128)(2,1)S(1)} collective-permute-done((bf16[64,64,128]{2,1,0:T(8,128)(2,1)}, bf16[64,64,128]{2,1,0:T(8,128)(2,1)S(1)}, u32[]{:S(2)}, u32[]{:S(2)}) %collective-permute-start) | collective-permute-done | bytes 1048608 | tf_op jit(solution)/shard_map/ppermute | solution.py:460
  238.1 0.0 copy-start
  238.1 1.0 copy-done
  239.1 4.0 %add_partial.1 = f32[64,128,128]{2,1,0:T(8,128)} custom-call(f32[64,128,128]{2,1,0:T(8,128)} %get-tuple-element.14.sum_ref, bf16[64,64,128]{2,1,0:T(8,128)(2,1)} %copy-done), custom_call_target="tpu_custom_call", output_to_operand_aliasing={{}: (0, {})} | custom-call | tf_op jit(solution)/shard_map/add_partial/pallas_call | solution.py:495
  (7 shorter events, 0.1 us)
Async XLA Ops:
  189.2 48.9 %collective-permute-start = (bf16[64,64,128]{2,1,0:T(8,128)(2,1)}, bf16[64,64,128]{2,1,0:T(8,128)(2,1)S(1)}, u32[]{:S(2)}, u32[]{:S(2)}) collective-permute-start(bf16[64,64,128]{2,1,0:T(8,128)(2,1)} %relay.1), channel_id=1, source_target_pairs={{0,4},{1,5},{2,6},{3,7},{4,0},{5,1},{6,2},{7,3},{8,12},{9,13},{10,... | collective-permute-start | bytes 3145736 | tf_op jit(solution)/shard_map/ppermute | solution.py:460
  238.1 1.0 copy-start

commit v5 on v4

--- a/solution.py
+++ b/solution.py
@@ -11,7 +11,7 @@
 SLOT_DEV = 64
 VSLOT_DEV = 16
 LANES = 128
-DIRECT = 64
+DIRECT = 32
 VMEM_LIMIT = 58 * 1024 * 1024
 MESH = pl.DeviceIdType.MESH
 
@@ -123,7 +123,8 @@
     aux,
     recv,
     relay,
-    auxrecv,
+    auxnear,
+    auxfar,
     auxrelay,
     sems,
     auxsems,
@@ -171,16 +172,10 @@
 
     def near_copies(j):
         device = near(j)
-        d = flat(device)
         return (
             remote(
-                send.at[pl.ds(d * room, room)],
-                recv.at[pl.ds(me * room, room)],
-                sems, 0, j, device,
-            ),
-            remote(
-                aux.at[pl.ds(d * auxrows, auxrows)],
-                auxrecv.at[pl.ds(me * auxrows, auxrows)],
+                aux.at[pl.ds(flat(device) * auxrows, auxrows)],
+                auxnear.at[pl.ds(mine * auxrows, auxrows)],
                 auxsems, 0, j, device,
             ),
         )
@@ -191,12 +186,12 @@
         return (
             remote(
                 send.at[pl.ds(d * room, room), pl.ds(0, direct)],
-                recv.at[pl.ds(me * room, room), pl.ds(0, direct)],
+                recv.at[pl.ds(mine * room, room)],
                 sems, 1, j, device,
             ),
             remote(
                 aux.at[pl.ds(d * auxrows, auxrows)],
-                auxrecv.at[pl.ds(me * auxrows, auxrows)],
+                auxfar.at[pl.ds(mine * auxrows, auxrows)],
                 auxsems, 1, j, device,
             ),
         )
@@ -237,20 +232,17 @@
     twin = flat(far(0))
     local = (
         pltpu.make_async_copy(
-            send.at[pl.ds(me * room, room)], recv.at[pl.ds(me * room, room)], own.at[0]
-        ),
-        pltpu.make_async_copy(
             aux.at[pl.ds(me * auxrows, auxrows)],
-            auxrecv.at[pl.ds(me * auxrows, auxrows)],
-            own.at[1],
+            auxnear.at[pl.ds(mine * auxrows, auxrows)],
+            own.at[0],
         ),
         pltpu.make_async_copy(
             send.at[pl.ds(twin * room, room), pl.ds(direct, tile - direct)],
             relay.at[pl.ds(mine * room, room)],
-            own.at[2],
+            own.at[1],
         ),
         pltpu.make_async_copy(
-            aux.at[pl.ds(twin * auxrows + vrows, 8)], auxrelay.at[pl.ds(mine * 8, 8)], own.at[3]
+            aux.at[pl.ds(twin * auxrows + vrows, 8)], auxrelay.at[pl.ds(mine * 8, 8)], own.at[2]
         ),
     )
     for copy in local:
@@ -266,6 +258,65 @@
             copy.wait()
 
 
+def swap_kernel(groups, columns, room, send, partial, recv, other, sems, own):
+    part = columns // 2
+    half = groups * part
+    g, c = lax.axis_index("grp"), lax.axis_index("blk")
+    base = (c // part) * part
+    inner = c % part
+    me, mine = g * columns + c, g * part + inner
+
+    def near(j):
+        return (g + j // part) % groups, base + (inner + j % part) % part
+
+    twin = (g, (c + part) % columns)
+    barrier = pltpu.get_barrier_semaphore()
+    pl.semaphore_signal(barrier, inc=1, device_id=twin, device_id_type=MESH)
+
+    @pl.loop(1, half)
+    def _(j):
+        pl.semaphore_signal(barrier, inc=1, device_id=near(j), device_id_type=MESH)
+
+    pl.semaphore_wait(barrier, half)
+
+    def near_copy(j):
+        device = near(j)
+        d = device[0] * columns + device[1]
+        return pltpu.make_async_remote_copy(
+            src_ref=send.at[pl.ds(d * room, room)],
+            dst_ref=recv.at[pl.ds(mine * room, room)],
+            send_sem=sems.at[0, j],
+            recv_sem=sems.at[1, j],
+            device_id=device,
+            device_id_type=MESH,
+        )
+
+    swap = pltpu.make_async_remote_copy(
+        src_ref=partial,
+        dst_ref=other,
+        send_sem=sems.at[0, 0],
+        recv_sem=sems.at[1, 0],
+        device_id=twin,
+        device_id_type=MESH,
+    )
+    swap.start()
+
+    @pl.loop(1, half)
+    def _(j):
+        near_copy(j).start()
+
+    local = pltpu.make_async_copy(
+        send.at[pl.ds(me * room, room)], recv.at[pl.ds(mine * room, room)], own.at[0]
+    )
+    local.start()
+    local.wait()
+    swap.wait()
+
+    @pl.loop(1, half)
+    def _(j):
+        near_copy(j).wait()
+
+
 def relay_kernel(group, room, ids, relay_ref, out_ref, total):
     step = pl.program_id(0)
 
@@ -289,52 +340,52 @@
 
 
 def sum_kernel(
-    group, room, vroom, vrows, direct, close, ids, recv_ref, aux_ref, out_ref, loads_ref
+    group,
+    room,
+    vroom,
+    vrows,
+    direct,
+    near_ids,
+    far_ids,
+    near_ref,
+    far_ref,
+    near_aux,
+    far_aux,
+    other_ref,
+    out_ref,
+    loads_ref,
 ):
-    step = pl.program_id(0)
     auxrows = vrows + 8
 
-    @pl.when(step == 0)
+    @pl.when(pl.program_id(0) == 0)
     def _():
-        out_ref[...] = jnp.zeros_like(out_ref)
+        out_ref[:, :direct, :] = jnp.zeros((SLOT_DEV, direct, LANES), jnp.float32)
+        out_ref[:, direct:, :] = other_ref[...].astype(jnp.float32)
         loads_ref[...] = jnp.zeros_like(loads_ref)
 
     for p in range(group):
         first = p * auxrows
-        whole = close[step * group + p] > 0
-
-        for v in range(vroom):
-            slot = ids[first + vrows + 1, v].astype(jnp.int32)
-
-            @pl.when(slot >= 0)
+
+        for ids, aux_ref in ((near_ids, near_aux), (far_ids, far_aux)):
+            for v in range(vroom):
+                slot = ids[first + vrows + 1, v].astype(jnp.int32)
+
+                @pl.when(slot >= 0)
+                def _():
+                    loads_ref[pl.ds(slot, 1), :] += aux_ref[pl.ds(first + v, 1), :]
+
+        @pl.loop(0, room)
+        def _(r):
+            target = near_ids[first + vrows, r].astype(jnp.int32)
+            beyond = far_ids[first + vrows, r].astype(jnp.int32)
+
+            @pl.when(target >= 0)
             def _():
-                loads_ref[pl.ds(slot, 1), :] += aux_ref[pl.ds(first + v, 1), :]
-
-        @pl.when(whole)
-        def _():
-            @pl.loop(0, room)
-            def _(r):
-                target = ids[first + vrows, r].astype(jnp.int32)
-
-                @pl.when(target >= 0)
-                def _():
-                    out_ref[target] += recv_ref[p * room + r].astype(jnp.float32)
-
-        @pl.when(jnp.logical_not(whole))
-        def _():
-            @pl.loop(0, room)
-            def _(r):
-                target = ids[first + vrows, r].astype(jnp.int32)
-
-                @pl.when(target >= 0)
-                def _():
-                    out_ref[target, :direct, :] += recv_ref[p * room + r, :direct, :].astype(
-                        jnp.float32
-                    )
-
-
-def add_kernel(sum_ref, far_ref, out_ref):
-    out_ref[...] = sum_ref[...] + far_ref[...].astype(jnp.float32)
+                out_ref[target] += near_ref[p * room + r].astype(jnp.float32)
+
+            @pl.when(beyond >= 0)
+            def _():
+                out_ref[beyond, :direct, :] += far_ref[p * room + r].astype(jnp.float32)
 
 
 def shards(
@@ -415,22 +466,23 @@
     )(counts, pos, vpos, inv_factor, coupling, boundary, load_int, load_bnd, table)
 
     half = peers // 2
-    recv, relay, auxrecv, auxrelay = pl.pallas_call(
+    far, relay, auxnear, auxfar, auxrelay = pl.pallas_call(
         functools.partial(
             exchange_kernel, peers // columns, columns, room, vrows, auxrows, DIRECT
         ),
         in_specs=[pl.BlockSpec(memory_space=pl.ANY)] * 2,
-        out_specs=[pl.BlockSpec(memory_space=pl.ANY)] * 4,
+        out_specs=[pl.BlockSpec(memory_space=pl.ANY)] * 5,
         out_shape=[
-            jax.ShapeDtypeStruct((peers * room, tile, tile), jnp.bfloat16),
+            jax.ShapeDtypeStruct((half * room, DIRECT, tile), jnp.bfloat16),
             jax.ShapeDtypeStruct((half * room, tile - DIRECT, tile), jnp.bfloat16),
-            jax.ShapeDtypeStruct((peers * auxrows, LANES), jnp.float32),
+            jax.ShapeDtypeStruct((half * auxrows, LANES), jnp.float32),
+            jax.ShapeDtypeStruct((half * auxrows, LANES), jnp.float32),
             jax.ShapeDtypeStruct((half * 8, LANES), jnp.float32),
         ],
         scratch_shapes=[
             pltpu.SemaphoreType.DMA((6, half)),
             pltpu.SemaphoreType.DMA((6, half)),
-            pltpu.SemaphoreType.DMA((4,)),
+            pltpu.SemaphoreType.DMA((3,)),
         ],
         compiler_params=pltpu.CompilerParams(
             collective_id=0, has_side_effects=True, vmem_limit_bytes=VMEM_LIMIT
@@ -456,28 +508,46 @@
         name="relay",
     )(auxrelay, relay)
 
-    part = columns // 2
-    other = lax.ppermute(partial, "blk", [(c, (c + part) % columns) for c in range(columns)])
-
-    source = jnp.arange(peers, dtype=jnp.int32) % columns
-    close = (source // part == lax.axis_index("blk") // part).astype(jnp.int32)
-    summed, loads = pl.pallas_call(
+    recv, other = pl.pallas_call(
+        functools.partial(swap_kernel, peers // columns, columns, room),
+        in_specs=[pl.BlockSpec(memory_space=pl.ANY)] * 2,
+        out_specs=[pl.BlockSpec(memory_space=pl.ANY)] * 2,
+        out_shape=[
+            jax.ShapeDtypeStruct((half * room, tile, tile), jnp.bfloat16),
+            jax.ShapeDtypeStruct(partial.shape, jnp.bfloat16),
+        ],
+        scratch_shapes=[
+            pltpu.SemaphoreType.DMA((2, half)),
+            pltpu.SemaphoreType.DMA((1,)),
+        ],
+        compiler_params=pltpu.CompilerParams(
+            collective_id=1, has_side_effects=True, vmem_limit_bytes=VMEM_LIMIT
+        ),
+        name="swap",
+    )(send, partial)
+
+    def ids_block():
+        return pl.BlockSpec((group * auxrows, LANES), lambda s: (s, 0), memory_space=pltpu.SMEM)
+
+    def aux_block():
+        return pl.BlockSpec((group * auxrows, LANES), lambda s: (s, 0))
+
+    assembled, loads = pl.pallas_call(
         functools.partial(sum_kernel, group, room, vroom, vrows, DIRECT),
-        grid_spec=pltpu.PrefetchScalarGridSpec(
-            num_scalar_prefetch=1,
-            grid=(peers // group,),
-            in_specs=[
-                pl.BlockSpec(
-                    (group * auxrows, LANES), lambda s, *_: (s, 0), memory_space=pltpu.SMEM
-                ),
-                pl.BlockSpec((group * room, tile, tile), lambda s, *_: (s, 0, 0)),
-                pl.BlockSpec((group * auxrows, LANES), lambda s, *_: (s, 0)),
-            ],
-            out_specs=[
-                pl.BlockSpec((SLOT_DEV, tile, tile), lambda s, *_: (0, 0, 0)),
-                pl.BlockSpec((VSLOT_DEV, LANES), whole),
-            ],
-        ),
+        grid=(half // group,),
+        in_specs=[
+            ids_block(),
+            ids_block(),
+            pl.BlockSpec((group * room, tile, tile), lambda s: (s, 0, 0)),
+            pl.BlockSpec((group * room, DIRECT, tile), lambda s: (s, 0, 0)),
+            aux_block(),
+            aux_block(),
+            pl.BlockSpec((SLOT_DEV, rest, tile), lambda s: (0, 0, 0)),
+        ],
+        out_specs=[
+            pl.BlockSpec((SLOT_DEV, tile, tile), lambda s: (0, 0, 0)),
+            pl.BlockSpec((VSLOT_DEV, LANES), whole),
+        ],
         out_shape=[
             jax.ShapeDtypeStruct((SLOT_DEV, tile, tile), jnp.float32),
             jax.ShapeDtypeStruct((VSLOT_DEV, LANES), jnp.float32),
@@ -485,28 +555,8 @@
         compiler_params=pltpu.CompilerParams(
             dimension_semantics=("arbitrary",), vmem_limit_bytes=VMEM_LIMIT
         ),
-        cost_estimate=pl.CostEstimate(
-            flops=peers * room * tile * tile, bytes_accessed=30_000_000, transcendentals=0
-        ),
         name="assemble",
-    )(close, auxrecv, recv, auxrecv)
-
-    strip = 16
-    assembled = pl.pallas_call(
-        add_kernel,
-        grid=(rest // strip,),
-        in_specs=[
-            pl.BlockSpec((SLOT_DEV, strip, tile), lambda s: (0, DIRECT // strip + s, 0)),
-            pl.BlockSpec((SLOT_DEV, strip, tile), lambda s: (0, s, 0)),
-        ],
-        out_specs=pl.BlockSpec((SLOT_DEV, strip, tile), lambda s: (0, DIRECT // strip + s, 0)),
-        out_shape=jax.ShapeDtypeStruct((SLOT_DEV, tile, tile), jnp.float32),
-        input_output_aliases={0: 0},
-        compiler_params=pltpu.CompilerParams(
-            dimension_semantics=("arbitrary",), vmem_limit_bytes=VMEM_LIMIT
-        ),
-        name="add_partial",
-    )(summed, other)
+    )(auxnear, auxfar, recv, far, auxnear, auxfar, other)
     return (assembled, loads)
 
 

time: 247 us -> 233 us (0.943)
  waiting for transfers between devices: 30.5 us -> 0 us
  Pallas kernels: 197 us -> 220 us
  starting transfers between devices: 4.75 us -> 0 us
    pallas_call x1, Pallas kernels: 3.97 us -> 97.2 us  [shards(): pl.pallas_call(functools.partial(swap_kernel, peers // columns, columns,...]
    pallas_call x1, Pallas kernels: 166 us -> 92.9 us  [shards(): pl.pallas_call(functools.partial(exchange_kernel, peers // columns, colum...]
    ppermute x1 -> x0, waiting for transfers between devices: 30.5 us -> none  [shards(): lax.ppermute(partial, 'blk', [(c, (c + part) % columns) for c in range(co...]
    pallas_call x1, Pallas kernels: 7.92 us -> 13 us  [shards(): pl.pallas_call(functools.partial(condense_kernel, emax, tiles), grid_spec...]
    ppermute x1 -> x0, starting transfers between devices: 4.75 us -> none  [shards(): lax.ppermute(partial, 'blk', [(c, (c + part) % columns) for c in range(co...]
    pallas_call x1, Pallas kernels: 13 us -> 9.92 us  [shards(): pl.pallas_call(functools.partial(sum_kernel, group, room, vroom, vrows, D...]
  transfers between devices with their start and end apart: 1 -> 0, of which waited for: 1 -> 0; matrix products, arithmetic and copies ran while one was open for 0% -> 0% of each run, Pallas kernels for 5% -> 0%
where the time goes in v5:
time: 233 us; the launch traced here: 229 us
  Pallas kernels  220 us (94%)
  other arithmetic  5.85 us (3%)
    pallas_call x1, Pallas kernels, shards(): pl.pallas_call(functools.partial(swap_kernel, peers // columns, columns,...  97.2 us
    pallas_call x1, Pallas kernels, shards(): pl.pallas_call(functools.partial(exchange_kernel, peers // columns, colum...  92.9 us
    pallas_call x1, Pallas kernels, shards(): pl.pallas_call(functools.partial(condense_kernel, emax, tiles), grid_spec...  13 us
    pallas_call x1, Pallas kernels, shards(): pl.pallas_call(functools.partial(sum_kernel, group, room, vroom, vrows, D...  9.92 us
    pallas_call x1, Pallas kernels, shards(): pl.pallas_call(functools.partial(relay_kernel, group, room), grid=(half /...  6.48 us

profile of v5, /device:TPU:11, one launch (start us, length us, event | category | flops | bytes accessed | tf_op | source)
XLA Modules:
  0.0 228.6 jit_solution(1941924997713365289)
XLA Ops:
  1.3 0.8 broadcast_in_dim.101
  2.1 0.8 broadcast_in_dim.93
  2.9 0.1 broadcast_in_dim.99
  3.0 0.1 broadcast_in_dim.91
  3.0 0.7 reduce
  3.8 0.1 reshape.143
  3.8 0.2 convert_reduce_fusion
  4.0 0.6 multiply_add_fusion.pos
  4.6 0.7 reduce.1
  5.3 0.1 reshape.144
  5.4 0.2 convert_reduce_fusion.1
  5.6 0.6 multiply_add_fusion.1.vpos
  6.1 0.1 iota_compare_fusion.4
  6.2 0.1 iota_compare_fusion.3
  6.3 0.3 select_reduce_fusion.1
  6.6 0.1 iota_compare_fusion.1
  6.7 1.4 select_reduce_fusion
  8.2 0.9 fusion.1.ids_ref
  9.1 13.0 %condense.1 = (bf16[320,128,128]{2,1,0:T(8,128)(2,1)}, f32[512,128]{1,0:T(8,128)}) custom-call(s32[1]{0:T(128)S(6)} %copy.12.counts, s32[216]{0:T(256)} %multiply_add_fusion.pos, s32[36]{0:T(128)} %multiply_add_fusion.1.vpos, bf16[6,384,384]{2,1,0:T(8,128)(2,1)} %factor_ref.1, bf16[6,384,768]{2,1,0:T(8,128)(2,1)} %couple_ref.1, ...), custom_call_target="tpu_custom_call" | custom-call | tf_op jit(solution)/shard_map/condense/pallas_call | solution.py:436
  22.1 92.9 %exchange.1 = (bf16[160,32,128]{2,1,0:T(8,128)(2,1)}, bf16[160,96,128]{2,1,0:T(8,128)(2,1)}, f32[256,128]{1,0:T(8,128)}, f32[256,128]{1,0:T(8,128)}, f32[128,128]{1,0:T(8,128)}) custom-call(bf16[320,128,128]{2,1,0:T(8,128)(2,1)} %get-tuple-element.11.send, f32[512,128]{1,0:T(8,128)} %get-tuple-element.12.aux), custom_call_target="tpu_custom_call" | custom-call | tf_op jit(solution)/shard_map/exchange/pallas_call | solution.py:469
  115.0 6.5 %relay.1.partial = bf16[64,96,128]{2,1,0:T(8,128)(2,1)} custom-call(f32[128,128]{1,0:T(8,128)} %get-tuple-element.15.ids, bf16[160,96,128]{2,1,0:T(8,128)(2,1)} %get-tuple-element.16.relay_ref), custom_call_target="tpu_custom_call" | custom-call | tf_op jit(solution)/shard_map/relay/pallas_call | solution.py:495
  121.5 97.2 %swap.1 = (bf16[160,128,128]{2,1,0:T(8,128)(2,1)}, bf16[64,96,128]{2,1,0:T(8,128)(2,1)}) custom-call(bf16[320,128,128]{2,1,0:T(8,128)(2,1)} %get-tuple-element.11.send, bf16[64,96,128]{2,1,0:T(8,128)(2,1)} %relay.1.partial), custom_call_target="tpu_custom_call" | custom-call | tf_op jit(solution)/shard_map/swap/pallas_call | solution.py:511
  218.7 9.9 %assemble.1 = (f32[64,128,128]{2,1,0:T(8,128)}, f32[16,128]{1,0:T(8,128)}) custom-call(f32[256,128]{1,0:T(8,128)} %get-tuple-element.13.near_ids.near_aux, f32[256,128]{1,0:T(8,128)} %get-tuple-element.14.far_ids.far_aux, bf16[160,128,128]{2,1,0:T(8,128)(2,1)} %get-tuple-element.17.near_ref, bf16[160,32,128]{2,1,0:T(8,128)(2,1)} %get-tuple-element.18.far_ref, ...), custom_call_target="tpu_custom_call" | custom-call | tf_op jit(solution)/shard_map/assemble/pallas_call | solution.py:535
  (7 shorter events, 0.0 us)
